TPU v7x, 512 devices: a whole 4x8x8 slice. The times are simulated.
512 devices in a mesh: gx: 16 (over x_hi, y), gy: 32 (over x_lo, z, core).
Axes of the slice: x: 4 (x_hi: 2, x_lo: 2; x = x_hi * 2 + x_lo), y: 8, z: 8, core: 2. Of those that a mesh axis runs over, the one named last changes fastest.
Arguments:
- velocity_term: float32 [32, 256, 2048], P(None, 'gy', 'gx'), may hold values from 0.03 to 0.18
- wave_before: float32 [32, 256, 2048], P(None, 'gy', 'gx'), may hold values from -2.4 to 2.4
- wave_now: float32 [32, 256, 2048], P(None, 'gy', 'gx'), may hold values from -2.4 to 2.4
- adjoint_later: float32 [32, 256, 2048], P(None, 'gy', 'gx'), may hold values from -4 to 4
- adjoint_next: float32 [32, 256, 2048], P(None, 'gy', 'gx'), may hold values from -4 to 4
- point_holder: int32 [131072, 1], P(('gx', 'gy')), may hold values from 0 to 15; in each aligned block of 256 rows (0 to 255, 256 to 511, ...) at most 64 rows name the same one
- point_cell: int32 [131072], P(('gx', 'gy')), may hold values from 0 to 32767
- coupling: float32 [65536], P(('gx', 'gy')), may hold values from 0.5 to 2
- observed: float32 [2, 65536], P(None, ('gx', 'gy')), may hold values from -4 to 4
Outputs:
- grad_velocity: float32 [32, 256, 2048], P(None, 'gy', 'gx')
- grad_coupling: float32 [65536], P(('gx', 'gy'))
- adjoint_early: float32 [32, 256, 2048], P(None, 'gy', 'gx')
- adjoint_middle: float32 [32, 256, 2048], P(None, 'gy', 'gx')
Inputs may be any that keep to these rules, and one draw needn't show every extreme that they name: `point_holder`: the 256 end points of one device lie in grid blocks with that device's index along gy; among them no holder is named more than 64 times, a bound that some block reaches. `point_cell`: A cell index inside the holder's block of 32 x 8 x 128 cells.
All inputs are finite; a program needn't handle non-finite values.
Results may differ from a plain program's by a relative error of at most 0.00002.
Values sent between devices are 32-bit elements; how exact they have to be, the bound alone decides.
A program may use at most 64 MiB of HBM per device.

v0:
```python
import jax
import jax.numpy as jnp
from jax import lax
from jax.sharding import PartitionSpec as P

STENCIL = (-205.0 / 72.0, 8.0 / 5.0, -1.0 / 5.0, 8.0 / 315.0, -1.0 / 560.0)


def with_halo(cells, sides, width):
    for axis, dim in sides:
        count = lax.axis_size(axis)
        ends = count - 1
        head = lax.slice_in_dim(cells, 0, width, axis=dim)
        tail = lax.slice_in_dim(cells, cells.shape[dim] - width, cells.shape[dim], axis=dim)
        cells = jnp.concatenate(
            [
                lax.ppermute(tail, axis, [(i, (i + 1) % count) for i in range(ends)]),
                cells,
                lax.ppermute(head, axis, [((i + 1) % count, i) for i in range(ends)]),
            ],
            axis=dim,
        )
    return cells


def laplace(padded):
    levels = padded.shape[0]
    rows_y = padded.shape[1] - 8
    cols_x = padded.shape[2] - 8
    deeper = jnp.pad(padded, ((4, 4), (0, 0), (0, 0)))

    def window(step_z, step_y, step_x):
        return deeper[
            4 + step_z : 4 + step_z + levels,
            4 + step_y : 4 + step_y + rows_y,
            4 + step_x : 4 + step_x + cols_x,
        ]

    summed = 3.0 * STENCIL[0] * window(0, 0, 0)
    for offset in range(1, 5):
        neighbours = window(offset, 0, 0) + window(-offset, 0, 0)
        neighbours = neighbours + window(0, offset, 0) + window(0, -offset, 0)
        neighbours = neighbours + window(0, 0, offset) + window(0, 0, -offset)
        summed = summed + STENCIL[offset] * neighbours
    return summed


def forward_laplace(field):
    return laplace(with_halo(field, (("gx", 2), ("gy", 1)), 4))


def adjoint_laplace(field):
    return laplace(with_halo(field, (("gx", 2), ("gy", 1)), 4))


def per_device(
    velocity_term,
    wave_before,
    wave_now,
    adjoint_later,
    adjoint_next,
    point_holder,
    point_cell,
    coupling,
    observed,
):
    laplace_one = forward_laplace(wave_now)
    wave_next = 2.0 * wave_now - wave_before + velocity_term * laplace_one
    laplace_two = forward_laplace(wave_next)
    wave_last = 2.0 * wave_next - wave_now + velocity_term * laplace_two
    flat_next = wave_next.reshape(-1)
    flat_last = wave_last.reshape(-1)
    cells_total = flat_next.shape[0]
    holder = point_holder[:, 0]
    points = point_cell.shape[0]
    channels = coupling.shape[0]
    groups = lax.axis_size("gx")
    capacity = min(points, 4 * points // groups)
    columns = jnp.arange(groups, dtype=jnp.int32)
    onehot = (holder[:, None] == columns[None, :]).astype(jnp.int32)
    slot_index = jnp.sum((jnp.cumsum(onehot, axis=0) - 1) * onehot, axis=1)
    request = jnp.full((groups, capacity), -1, jnp.int32).at[holder, slot_index].set(point_cell)
    received = lax.all_to_all(request, "gx", split_axis=0, concat_axis=0, tiled=True)
    is_valid = received >= 0
    target = jnp.maximum(received, 0)
    picked_two = jnp.where(is_valid, flat_next[target], 0.0)
    picked_last = jnp.where(is_valid, flat_last[target], 0.0)
    back_two = lax.all_to_all(picked_two, "gx", split_axis=0, concat_axis=0, tiled=True)
    back_last = lax.all_to_all(picked_last, "gx", split_axis=0, concat_axis=0, tiled=True)
    sample_two = back_two[holder, slot_index]
    sample_last = back_last[holder, slot_index]
    ends_two = sample_two.reshape(channels, 2)
    ends_last = sample_last.reshape(channels, 2)
    diff_two = ends_two[:, 1] - ends_two[:, 0]
    diff_last = ends_last[:, 1] - ends_last[:, 0]
    error_two = coupling * diff_two - observed[0]
    error_last = coupling * diff_last - observed[1]
    grad_coupling = error_two * diff_two + error_last * diff_last
    strength_two = coupling * error_two
    strength_last = coupling * error_last
    sources = jnp.stack(
        [
            jnp.stack([-strength_two, strength_two], axis=1).reshape(points),
            jnp.stack([-strength_last, strength_last], axis=1).reshape(points),
        ]
    )
    payload = jnp.zeros((2, groups, capacity), jnp.float32).at[:, holder, slot_index].set(sources)
    arrived_sources = lax.all_to_all(payload, "gx", split_axis=1, concat_axis=1, tiled=True)
    target = jnp.maximum(received, 0).reshape(-1)
    injected = (
        jnp.zeros((2, cells_total), jnp.float32).at[:, target].add(arrived_sources.reshape(2, -1))
    )
    inject_two = injected[0].reshape(velocity_term.shape)
    inject_last = injected[1].reshape(velocity_term.shape)
    adjoint_three = adjoint_later + inject_last
    level_two = adjoint_next + inject_two
    adjoint_middle = (
        level_two + 2.0 * adjoint_three + adjoint_laplace(velocity_term * adjoint_three)
    )
    adjoint_early = (
        -adjoint_three + 2.0 * adjoint_middle + adjoint_laplace(velocity_term * adjoint_middle)
    )
    grad_velocity = adjoint_three * laplace_two + adjoint_middle * laplace_one
    return (grad_velocity, grad_coupling, adjoint_early, adjoint_middle)


def solution(mesh):
    return jax.shard_map(
        per_device,
        mesh=mesh,
        in_specs=(
            P(None, "gy", "gx"),
            P(None, "gy", "gx"),
            P(None, "gy", "gx"),
            P(None, "gy", "gx"),
            P(None, "gy", "gx"),
            P(("gx", "gy"), None),
            P(("gx", "gy")),
            P(("gx", "gy")),
            P(None, ("gx", "gy")),
        ),
        out_specs=(P(None, "gy", "gx"), P(("gx", "gy")), P(None, "gy", "gx"), P(None, "gy", "gx")),
        check_vma=False,
    )
```

profile of v0, /device:TPU:6, one launch (start us, length us, event | category | flops | bytes accessed | tf_op | source)
XLA Modules:
  0.0 264.4 jit_solution(514275005858386257)
XLA Ops:
  4.2 36.0 %scatter_fusion = s32[16,64]{1,0:T(8,128)} fusion(s32[16,64]{1,0:T(8,128)} %broadcast_in_dim.12, s32[256]{0:T(256)S(1)} %bitcast.72, s32[256]{0:T(256)} %param.15), kind=kCustom, calls=%fused_computation.4 | custom fusion | bytes 5120 | tf_op jit(solution)/shard_map/scatter | solution.py:82
  40.3 10.3 %all-to-all-start = ((s32[16,1,64]{2,1,0:T(1,128)}), s32[16,1,64]{2,1,0:T(1,128)S(1)}, u32[]{:S(2)}, u32[]{:S(2)}) async-start(s32[16,1,64]{2,1,0:T(1,128)} %bitcast.6), calls=%async_computation | async-start | bytes 16384 | tf_op jit(solution)/shard_map/all_to_all | solution.py:83
  51.6 4.6 %collective-permute-start.1 = (f32[32,8,4]{2,1,0:T(8,128)S(1)}, f32[32,8,4]{2,1,0:T(8,128)S(1)}, u32[]{:S(2)}, u32[]{:S(2)}) collective-permute-start(f32[32,8,4]{2,1,0:T(8,128)S(1)} %get-tuple-element.38), channel_id=1, source_target_pairs={{32,0},{64,32},{96,64},{128,96},{160,128},{192,160},{224,192},{256... | collective-permute-start | bytes 12296 | tf_op jit(solution)/shard_map/ppermute | solution.py:19
  56.2 1.9 collective-permute-start
  59.1 7.6 %collective-permute-done = f32[32,8,4]{2,1,0:T(8,128)S(1)} collective-permute-done((f32[32,8,4]{2,1,0:T(8,128)S(1)}, f32[32,8,4]{2,1,0:T(8,128)S(1)}, u32[]{:S(2)}, u32[]{:S(2)}) %collective-permute-start) | collective-permute-done | bytes 4128 | tf_op jit(solution)/shard_map/ppermute | solution.py:17
  67.8 8.8 %collective-permute-start.3 = (f32[32,4,136]{2,1,0:T(4,128)S(1)}, f32[32,4,136]{2,1,0:T(4,128)S(1)}, u32[]{:S(2)}, u32[]{:S(2)}) collective-permute-start(f32[32,4,136]{2,1,0:T(4,128)S(1)} %get-tuple-element.30), channel_id=1, source_target_pairs={{1,0},{2,1},{3,2},{4,3},{5,4},{6,5},{7,6},{8,7},{9,8},{10,9},{11,1... | collective-permute-start | bytes 208904 | tf_op jit(solution)/shard_map/ppermute | solution.py:19
  76.6 1.9 collective-permute-start.2
  79.1 5.9 %collective-permute-done.2 = f32[32,4,136]{2,1,0:T(4,128)S(1)} collective-permute-done((f32[32,4,136]{2,1,0:T(4,128)S(1)}, f32[32,4,136]{2,1,0:T(4,128)S(1)}, u32[]{:S(2)}, u32[]{:S(2)}) %collective-permute-start.2) | collective-permute-done | bytes 69664 | tf_op jit(solution)/shard_map/ppermute | solution.py:17
  87.5 2.3 multiply_add_fusion.1
  89.9 2.4 collective-permute-start.5
  92.3 3.5 %collective-permute-start.4 = (f32[32,8,4]{2,1,0:T(8,128)S(1)}, f32[32,8,4]{2,1,0:T(8,128)S(1)}, u32[]{:S(2)}, u32[]{:S(2)}) collective-permute-start(f32[32,8,4]{2,1,0:T(8,128)S(1)} %get-tuple-element.37), channel_id=1, source_target_pairs={{0,32},{32,64},{64,96},{96,128},{128,160},{160,192},{192,224},{224... | collective-permute-start | bytes 12296 | tf_op jit(solution)/shard_map/ppermute | solution.py:17
  96.8 6.0 %collective-permute-done.4 = f32[32,8,4]{2,1,0:T(8,128)S(1)} collective-permute-done((f32[32,8,4]{2,1,0:T(8,128)S(1)}, f32[32,8,4]{2,1,0:T(8,128)S(1)}, u32[]{:S(2)}, u32[]{:S(2)}) %collective-permute-start.4) | collective-permute-done | bytes 4128 | tf_op jit(solution)/shard_map/ppermute | solution.py:17
  105.0 2.4 collective-permute-start.6
  107.4 6.2 %gather_fusion = f32[1024]{0:T(1024)S(1)} fusion(f32[32768]{0:T(1024)S(1)} %bitcast.69, s32[1024]{0:T(1024)S(1)} %broadcast_clamp_fusion), kind=kCustom, calls=%fused_computation | custom fusion | bytes 12288 | tf_op jit(solution)/shard_map/gather | solution.py:86
  115.5 6.2 %gather_fusion.2 = f32[1024]{0:T(1024)S(1)} fusion(f32[32768]{0:T(1024)S(1)} %get-tuple-element.10, s32[1024]{0:T(1024)S(1)} %broadcast_clamp_fusion), kind=kCustom, calls=%fused_computation.2 | custom fusion | bytes 12288 | tf_op jit(solution)/shard_map/gather | solution.py:87
  122.3 11.7 %all_to_all.32 = f32[16,1,64]{2,1,0:T(1,128)S(1)} all-to-all(f32[16,1,64]{2,1,0:T(1,128)S(1)} %get-tuple-element.40), channel_id=1, replica_groups=mesh['gx'=16,'gy'=32] {'gx'}, dimensions={0} | all-to-all | bytes 8192 | tf_op jit(solution)/shard_map/all_to_all | solution.py:88
  134.0 6.3 %all-to-all-start.2 = ((f32[16,1,64]{2,1,0:T(1,128)}), f32[16,1,64]{2,1,0:T(1,128)S(1)}, u32[]{:S(2)}, u32[]{:S(2)}) async-start(f32[16,1,64]{2,1,0:T(1,128)} %get-tuple-element.41), calls=%async_computation.2 | async-start | bytes 16384 | tf_op jit(solution)/shard_map/all_to_all | solution.py:89
  140.3 1.9 gather_fusion.1
  142.3 5.1 %all-to-all-done.2 = f32[16,1,64]{2,1,0:T(1,128)S(1)} async-done(((f32[16,1,64]{2,1,0:T(1,128)}), f32[16,1,64]{2,1,0:T(1,128)S(1)}, u32[]{:S(2)}, u32[]{:S(2)}) %all-to-all-start.2) | async-done | bytes 4128 | tf_op jit(solution)/shard_map/all_to_all | solution.py:89
  147.4 1.9 gather_fusion.3
  151.2 12.2 %scatter_fusion.1 = f32[2,16,64]{0,2,1:T(8,128)S(1)} fusion(f32[2,16,64]{0,2,1:T(8,128)S(1)} %broadcast_in_dim.13, s32[256]{0:T(256)S(1)} %bitcast.73, f32[256,2]{1,0:T(8,128)S(1)} %copy.31), kind=kCustom, calls=%fused_computation.5 | custom fusion | bytes 8192 | tf_op jit(solution)/shard_map/scatter | solution.py:107
  163.8 12.5 %all_to_all.33 = f32[16,1,128]{2,1,0:T(1,128)S(1)} all-to-all(f32[16,1,128]{2,1,0:T(1,128)S(1)} %reshape.165), channel_id=1, replica_groups=mesh['gx'=16,'gy'=32] {'gx'}, dimensions={0} | all-to-all | bytes 16384 | tf_op jit(solution)/shard_map/all_to_all | solution.py:108
  177.9 13.1 %scatter_custom_fusion.2 = f32[2,32768]{0,1:T(8,128)} fusion(s32[1024]{0:T(1024)S(1)} %reshape.138, f32[1024,2]{1,0:T(8,128)S(1)} %copy.34, f32[]{:T(128)} %constant.11.clone.1), kind=kCustom, calls=%fused_computation.9 | custom fusion | flops 2048 | bytes 262148 | tf_op jit(solution)/shard_map/scatter-add | solution.py:111
  191.0 19.2 %slice_reduce_fusion = (f32[32768]{0:T(1024)S(1)}, f32[32768]{0:T(1024)S(1)}) fusion(f32[2,32768]{0,1:T(8,128)} %scatter_custom_fusion.2), kind=kLoop, calls=%fused_computation.7 | loop fusion | bytes 524288 | tf_op jit(solution)/shard_map/slice | solution.py:113
  210.4 5.7 %collective-permute-start.9 = (f32[32,8,4]{2,1,0:T(8,128)S(1)}, f32[32,8,4]{2,1,0:T(8,128)S(1)}, u32[]{:S(2)}, u32[]{:S(2)}) collective-permute-start(f32[32,8,4]{2,1,0:T(8,128)S(1)} %get-tuple-element.34), channel_id=1, source_target_pairs={{32,0},{64,32},{96,64},{128,96},{160,128},{192,160},{224,192},{256... | collective-permute-start | bytes 12296 | tf_op jit(solution)/shard_map/ppermute | solution.py:19
  218.5 8.0 %collective-permute-done.8 = f32[32,8,4]{2,1,0:T(8,128)S(1)} collective-permute-done((f32[32,8,4]{2,1,0:T(8,128)S(1)}, f32[32,8,4]{2,1,0:T(8,128)S(1)}, u32[]{:S(2)}, u32[]{:S(2)}) %collective-permute-start.8) | collective-permute-done | bytes 4128 | tf_op jit(solution)/shard_map/ppermute | solution.py:17
  228.7 2.4 collective-permute-start.10
  231.2 5.9 %collective-permute-done.10 = f32[32,4,136]{2,1,0:T(4,128)S(1)} collective-permute-done((f32[32,4,136]{2,1,0:T(4,128)S(1)}, f32[32,4,136]{2,1,0:T(4,128)S(1)}, u32[]{:S(2)}, u32[]{:S(2)}) %collective-permute-start.10) | collective-permute-done | bytes 69664 | tf_op jit(solution)/shard_map/ppermute | solution.py:17
  240.9 3.9 %collective-permute-start.12 = (f32[32,8,4]{2,1,0:T(8,128)S(1)}, f32[32,8,4]{2,1,0:T(8,128)S(1)}, u32[]{:S(2)}, u32[]{:S(2)}) collective-permute-start(f32[32,8,4]{2,1,0:T(8,128)S(1)} %get-tuple-element.33), channel_id=1, source_target_pairs={{0,32},{32,64},{64,96},{96,128},{128,160},{160,192},{192,224},{224... | collective-permute-start | bytes 12296 | tf_op jit(solution)/shard_map/ppermute | solution.py:17
  245.9 5.5 %collective-permute-done.12 = f32[32,8,4]{2,1,0:T(8,128)S(1)} collective-permute-done((f32[32,8,4]{2,1,0:T(8,128)S(1)}, f32[32,8,4]{2,1,0:T(8,128)S(1)}, u32[]{:S(2)}, u32[]{:S(2)}) %collective-permute-start.12) | collective-permute-done | bytes 4128 | tf_op jit(solution)/shard_map/ppermute | solution.py:17
  253.5 2.4 collective-permute-start.14
  256.6 5.3 %collective-permute-done.14 = f32[32,4,136]{2,1,0:T(4,128)S(1)} collective-permute-done((f32[32,4,136]{2,1,0:T(4,128)S(1)}, f32[32,4,136]{2,1,0:T(4,128)S(1)}, u32[]{:S(2)}, u32[]{:S(2)}) %collective-permute-start.14) | collective-permute-done | bytes 69664 | tf_op jit(solution)/shard_map/ppermute | solution.py:17
  (91 shorter events, 34.2 us)
Async XLA Ops:
  0.6 113.7 %copy-start = (f32[32,8,128]{2,1,0:T(8,128)S(1)}, f32[32,8,128]{2,1,0:T(8,128)}, u32[]{:S(2)}) copy-start(f32[32,8,128]{2,1,0:T(8,128)} %param.11) | copy-start | bytes 393220
  0.6 113.7 %copy-start.1 = (f32[32,8,128]{2,1,0:T(8,128)S(1)}, f32[32,8,128]{2,1,0:T(8,128)}, u32[]{:S(2)}) copy-start(f32[32,8,128]{2,1,0:T(8,128)} %param.9) | copy-start | bytes 393220
  40.3 55.5 %all-to-all-start = ((s32[16,1,64]{2,1,0:T(1,128)}), s32[16,1,64]{2,1,0:T(1,128)S(1)}, u32[]{:S(2)}, u32[]{:S(2)}) async-start(s32[16,1,64]{2,1,0:T(1,128)} %bitcast.6), calls=%async_computation | async-start | bytes 16384 | tf_op jit(solution)/shard_map/all_to_all | solution.py:83
  51.6 7.4 %collective-permute-start.1 = (f32[32,8,4]{2,1,0:T(8,128)S(1)}, f32[32,8,4]{2,1,0:T(8,128)S(1)}, u32[]{:S(2)}, u32[]{:S(2)}) collective-permute-start(f32[32,8,4]{2,1,0:T(8,128)S(1)} %get-tuple-element.38), channel_id=1, source_target_pairs={{32,0},{64,32},{96,64},{128,96},{160,128},{192,160},{224,192},{256... | collective-permute-start | bytes 12296 | tf_op jit(solution)/shard_map/ppermute | solution.py:19
  56.2 10.5 %collective-permute-start = (f32[32,8,4]{2,1,0:T(8,128)S(1)}, f32[32,8,4]{2,1,0:T(8,128)S(1)}, u32[]{:S(2)}, u32[]{:S(2)}) collective-permute-start(f32[32,8,4]{2,1,0:T(8,128)S(1)} %get-tuple-element.39), channel_id=1, source_target_pairs={{0,32},{32,64},{64,96},{96,128},{128,160},{160,192},{192,224},{224... | collective-permute-start | bytes 12296 | tf_op jit(solution)/shard_map/ppermute | solution.py:17
  67.8 11.3 %collective-permute-start.3 = (f32[32,4,136]{2,1,0:T(4,128)S(1)}, f32[32,4,136]{2,1,0:T(4,128)S(1)}, u32[]{:S(2)}, u32[]{:S(2)}) collective-permute-start(f32[32,4,136]{2,1,0:T(4,128)S(1)} %get-tuple-element.30), channel_id=1, source_target_pairs={{1,0},{2,1},{3,2},{4,3},{5,4},{6,5},{7,6},{8,7},{9,8},{10,9},{11,1... | collective-permute-start | bytes 208904 | tf_op jit(solution)/shard_map/ppermute | solution.py:19
  76.6 8.4 %collective-permute-start.2 = (f32[32,4,136]{2,1,0:T(4,128)S(1)}, f32[32,4,136]{2,1,0:T(4,128)S(1)}, u32[]{:S(2)}, u32[]{:S(2)}) collective-permute-start(f32[32,4,136]{2,1,0:T(4,128)S(1)} %get-tuple-element.31), channel_id=1, source_target_pairs={{0,1},{1,2},{2,3},{3,4},{4,5},{5,6},{6,7},{7,8},{8,9},{9,10},{10,1... | collective-permute-start | bytes 208904 | tf_op jit(solution)/shard_map/ppermute | solution.py:17
  78.5 71.4 %copy-start.5 = (f32[2,128]{1,0:T(2,128)S(1)}, f32[2,128]{1,0:T(2,128)}, u32[]{:S(2)}) copy-start(f32[2,128]{1,0:T(2,128)} %param.17) | copy-start | bytes 3076
  78.6 71.4 %copy-start.6 = (f32[128]{0:T(128)S(1)}, f32[128]{0:T(128)}, u32[]{:S(2)}) copy-start(f32[128]{0:T(128)} %param.16) | copy-start | bytes 1540
  89.9 6.9 %collective-permute-start.5 = (f32[32,8,4]{2,1,0:T(8,128)S(1)}, f32[32,8,4]{2,1,0:T(8,128)S(1)}, u32[]{:S(2)}, u32[]{:S(2)}) collective-permute-start(f32[32,8,4]{2,1,0:T(8,128)S(1)} %get-tuple-element.36), channel_id=1, source_target_pairs={{32,0},{64,32},{96,64},{128,96},{160,128},{192,160},{224,192},{256... | collective-permute-start | bytes 12296 | tf_op jit(solution)/shard_map/ppermute | solution.py:19
  92.3 10.5 %collective-permute-start.4 = (f32[32,8,4]{2,1,0:T(8,128)S(1)}, f32[32,8,4]{2,1,0:T(8,128)S(1)}, u32[]{:S(2)}, u32[]{:S(2)}) collective-permute-start(f32[32,8,4]{2,1,0:T(8,128)S(1)} %get-tuple-element.37), channel_id=1, source_target_pairs={{0,32},{32,64},{64,96},{96,128},{128,160},{160,192},{192,224},{224... | collective-permute-start | bytes 12296 | tf_op jit(solution)/shard_map/ppermute | solution.py:17
  103.0 10.6 %collective-permute-start.7 = (f32[32,4,136]{2,1,0:T(4,128)S(1)}, f32[32,4,136]{2,1,0:T(4,128)S(1)}, u32[]{:S(2)}, u32[]{:S(2)}) collective-permute-start(f32[32,4,136]{2,1,0:T(4,128)S(1)} %get-tuple-element.28), channel_id=1, source_target_pairs={{1,0},{2,1},{3,2},{4,3},{5,4},{6,5},{7,6},{8,7},{9,8},{10,9},{11,1... | collective-permute-start | bytes 208904 | tf_op jit(solution)/shard_map/ppermute | solution.py:19
  105.0 8.7 %collective-permute-start.6 = (f32[32,4,136]{2,1,0:T(4,128)S(1)}, f32[32,4,136]{2,1,0:T(4,128)S(1)}, u32[]{:S(2)}, u32[]{:S(2)}) collective-permute-start(f32[32,4,136]{2,1,0:T(4,128)S(1)} %get-tuple-element.29), channel_id=1, source_target_pairs={{0,1},{1,2},{2,3},{3,4},{4,5},{5,6},{6,7},{7,8},{8,9},{9,10},{10,1... | collective-permute-start | bytes 208904 | tf_op jit(solution)/shard_map/ppermute | solution.py:17
  134.0 13.3 %all-to-all-start.2 = ((f32[16,1,64]{2,1,0:T(1,128)}), f32[16,1,64]{2,1,0:T(1,128)S(1)}, u32[]{:S(2)}, u32[]{:S(2)}) async-start(f32[16,1,64]{2,1,0:T(1,128)} %get-tuple-element.41), calls=%async_computation.2 | async-start | bytes 16384 | tf_op jit(solution)/shard_map/all_to_all | solution.py:89
  191.0 19.2 %copy-start.3 = (f32[32,8,128]{2,1,0:T(8,128)S(1)}, f32[32,8,128]{2,1,0:T(8,128)}, u32[]{:S(2)}) copy-start(f32[32,8,128]{2,1,0:T(8,128)} %param.12) | copy-start | bytes 393220
  191.0 46.7 %copy-start.4 = (f32[32,8,128]{2,1,0:T(8,128)S(1)}, f32[32,8,128]{2,1,0:T(8,128)}, u32[]{:S(2)}) copy-start(f32[32,8,128]{2,1,0:T(8,128)} %param.13) | copy-start | bytes 393220
  210.4 8.2 %collective-permute-start.9 = (f32[32,8,4]{2,1,0:T(8,128)S(1)}, f32[32,8,4]{2,1,0:T(8,128)S(1)}, u32[]{:S(2)}, u32[]{:S(2)}) collective-permute-start(f32[32,8,4]{2,1,0:T(8,128)S(1)} %get-tuple-element.34), channel_id=1, source_target_pairs={{32,0},{64,32},{96,64},{128,96},{160,128},{192,160},{224,192},{256... | collective-permute-start | bytes 12296 | tf_op jit(solution)/shard_map/ppermute | solution.py:19
  216.0 10.5 %collective-permute-start.8 = (f32[32,8,4]{2,1,0:T(8,128)S(1)}, f32[32,8,4]{2,1,0:T(8,128)S(1)}, u32[]{:S(2)}, u32[]{:S(2)}) collective-permute-start(f32[32,8,4]{2,1,0:T(8,128)S(1)} %get-tuple-element.35), channel_id=1, source_target_pairs={{0,32},{32,64},{64,96},{96,128},{128,160},{160,192},{192,224},{224... | collective-permute-start | bytes 12296 | tf_op jit(solution)/shard_map/ppermute | solution.py:17
  226.7 4.4 %collective-permute-start.11 = (f32[32,4,136]{2,1,0:T(4,128)S(1)}, f32[32,4,136]{2,1,0:T(4,128)S(1)}, u32[]{:S(2)}, u32[]{:S(2)}) collective-permute-start(f32[32,4,136]{2,1,0:T(4,128)S(1)} %get-tuple-element.26), channel_id=1, source_target_pairs={{1,0},{2,1},{3,2},{4,3},{5,4},{6,5},{7,6},{8,7},{9,8},{10,9},{11,1... | collective-permute-start | bytes 208904 | tf_op jit(solution)/shard_map/ppermute | solution.py:19
  228.7 8.4 %collective-permute-start.10 = (f32[32,4,136]{2,1,0:T(4,128)S(1)}, f32[32,4,136]{2,1,0:T(4,128)S(1)}, u32[]{:S(2)}, u32[]{:S(2)}) collective-permute-start(f32[32,4,136]{2,1,0:T(4,128)S(1)} %get-tuple-element.27), channel_id=1, source_target_pairs={{0,1},{1,2},{2,3},{3,4},{4,5},{5,6},{6,7},{7,8},{8,9},{9,10},{10,1... | collective-permute-start | bytes 208904 | tf_op jit(solution)/shard_map/ppermute | solution.py:17
  238.9 25.5 %copy-start.2 = (f32[32,8,128]{2,1,0:T(8,128)}, f32[32,8,128]{2,1,0:T(8,128)S(1)}, u32[]{:S(2)}) copy-start(f32[32,8,128]{2,1,0:T(8,128)S(1)} %get-tuple-element.7) | copy-start | bytes 393220
  239.0 6.9 %collective-permute-start.13 = (f32[32,8,4]{2,1,0:T(8,128)S(1)}, f32[32,8,4]{2,1,0:T(8,128)S(1)}, u32[]{:S(2)}, u32[]{:S(2)}) collective-permute-start(f32[32,8,4]{2,1,0:T(8,128)S(1)} %get-tuple-element.32), channel_id=1, source_target_pairs={{32,0},{64,32},{96,64},{128,96},{160,128},{192,160},{224,192},{256... | collective-permute-start | bytes 12296 | tf_op jit(solution)/shard_map/ppermute | solution.py:19
  240.9 10.5 %collective-permute-start.12 = (f32[32,8,4]{2,1,0:T(8,128)S(1)}, f32[32,8,4]{2,1,0:T(8,128)S(1)}, u32[]{:S(2)}, u32[]{:S(2)}) collective-permute-start(f32[32,8,4]{2,1,0:T(8,128)S(1)} %get-tuple-element.33), channel_id=1, source_target_pairs={{0,32},{32,64},{64,96},{96,128},{128,160},{160,192},{192,224},{224... | collective-permute-start | bytes 12296 | tf_op jit(solution)/shard_map/ppermute | solution.py:17
  251.6 5.0 %collective-permute-start.15 = (f32[32,4,136]{2,1,0:T(4,128)S(1)}, f32[32,4,136]{2,1,0:T(4,128)S(1)}, u32[]{:S(2)}, u32[]{:S(2)}) collective-permute-start(f32[32,4,136]{2,1,0:T(4,128)S(1)} %get-tuple-element.24), channel_id=1, source_target_pairs={{1,0},{2,1},{3,2},{4,3},{5,4},{6,5},{7,6},{8,7},{9,8},{10,9},{11,1... | collective-permute-start | bytes 208904 | tf_op jit(solution)/shard_map/ppermute | solution.py:19
  253.5 8.4 %collective-permute-start.14 = (f32[32,4,136]{2,1,0:T(4,128)S(1)}, f32[32,4,136]{2,1,0:T(4,128)S(1)}, u32[]{:S(2)}, u32[]{:S(2)}) collective-permute-start(f32[32,4,136]{2,1,0:T(4,128)S(1)} %get-tuple-element.25), channel_id=1, source_target_pairs={{0,1},{1,2},{2,3},{3,4},{4,5},{5,6},{6,7},{7,8},{8,9},{9,10},{10,1... | collective-permute-start | bytes 208904 | tf_op jit(solution)/shard_map/ppermute | solution.py:17
where the time goes:
time: 266 us; the launch traced here: 264 us
  local copies, waits for them, and re-layouts  89.3 us (34%)
  starting transfers between devices  65.9 us (25%)
  waiting for transfers between devices  52.4 us (20%)
  other arithmetic  31.3 us (12%)
  blocking collectives  24.3 us (9%)
    ppermute x8, waiting for transfers between devices, with_halo(): lax.ppermute(tail, axis, [(i, (i + 1) % count) for i in range(ends)])  44.2 us
    scatter x1, local copies, waits for them, and re-layouts, per_device(): jnp.full((groups, capacity), -1, jnp.int32).at[holder, slot_index]  36 us
    ppermute x8, starting transfers between devices, with_halo(): lax.ppermute(head, axis, [((i + 1) % count, i) for i in range(ends)])  29.1 us
    ppermute x8, starting transfers between devices, with_halo(): lax.ppermute(tail, axis, [(i, (i + 1) % count) for i in range(ends)])  20.4 us
    slice x1, local copies, waits for them, and re-layouts, per_device(): inject_two = injected[0].reshape(velocity_term.shape)  19.2 us
    scatter-add x1, other arithmetic, per_device(): jnp.zeros((2, cells_total), jnp.float32).at[:, target]  13.1 us
    all_to_all x1, blocking collectives, per_device(): lax.all_to_all(payload, 'gx', split_axis=1, concat_axis=1, tiled=True)  12.5 us
    scatter x2, local copies, waits for them, and re-layouts, per_device(): jnp.zeros((2, groups, capacity), jnp.float32).at[:, holder, slot_index]  12.5 us
  transfers between devices with their start and end apart: 18, of which 13 were waited for; matrix products, arithmetic and copies ran while one was open for 6% of the time, Pallas kernels for 0%

commit v1 on v0

v1 whole, which is shorter than its diff:
```python
import functools

import jax
import jax.numpy as jnp
from jax import lax
from jax.experimental import pallas as pl
from jax.experimental.pallas import tpu as pltpu
from jax.sharding import PartitionSpec as P

STENCIL = (-205.0 / 72.0, 8.0 / 5.0, -1.0 / 5.0, 8.0 / 315.0, -1.0 / 560.0)
MESH = pl.DeviceIdType.MESH
F32 = jnp.float32
BF16 = jnp.bfloat16
PAD = 4
STEP_Z = 4
EDGE = 8


def iota(shape, dim):
    return lax.broadcasted_iota(jnp.int32, shape, dim)


def split3(value):
    high = value.astype(BF16)
    rest = value - high.astype(F32)
    mid = rest.astype(BF16)
    low = (rest - mid.astype(F32)).astype(BF16)
    return high, mid, low


def nt(a, b):
    return lax.dot_general(a, b, (((1,), (1,)), ((), ())), preferred_element_type=F32)


def nn(a, b):
    return lax.dot_general(a, b, (((1,), (0,)), ((), ())), preferred_element_type=F32)


def kernel(
    groups,
    rows,
    vt_ref,
    wb_ref,
    wn_ref,
    al_ref,
    an_ref,
    hold_ref,
    cell_ref,
    coup_ref,
    obs_ref,
    gv_ref,
    gc_ref,
    ae_ref,
    am_ref,
    field,
    lap,
    last,
    adj3,
    y_halo,
    x_send,
    x_recv,
    x_halo,
    match,
    at_row,
    at_lane,
    out_box,
    in_box,
    face_send,
    face_recv,
    box_send,
    box_recv,
):
    nz = vt_ref.shape[0]
    per_part = 128 // EDGE
    parts = x_send.shape[1]
    cap = 64
    slots = groups * cap
    points = hold_ref.shape[1]
    gx = lax.axis_index("gx")
    gy = lax.axis_index("gy")
    x_prev, x_next = lax.rem(gx + groups - 1, groups), lax.rem(gx + 1, groups)
    y_prev, y_next = lax.rem(gy + rows - 1, rows), lax.rem(gy + 1, rows)

    barrier = pltpu.get_barrier_semaphore()

    def greet(d, carry):
        pl.semaphore_signal(
            barrier, inc=1, device_id=(lax.rem(gx + d, groups), gy), device_id_type=MESH
        )
        return carry

    lax.fori_loop(1, groups, greet, 0)
    for other in (y_prev, y_next):
        pl.semaphore_signal(barrier, inc=1, device_id=(gx, other), device_id_type=MESH)

    lane = iota((8, 128), 1)
    sub = iota((8, 128), 0)

    def pack(k):
        for part in range(parts):
            packed = None
            for i in range(per_part):
                turned = pltpu.roll(
                    field[k, PAD + part * per_part + i], (EDGE * i + PAD) % 128, 1
                )
                packed = (
                    turned if packed is None else jnp.where(lane // EDGE == i, turned, packed)
                )
            x_send[k, part] = packed

    def face_copies(k):
        inner = pl.ds(PAD, nz)
        return (
            pltpu.make_async_remote_copy(
                field.at[k, inner, pl.ds(0, 4)],
                y_halo.at[k, :, pl.ds(0, 4)],
                face_send.at[k, 0],
                face_recv.at[k, 0],
                device_id=(gx, y_prev),
                device_id_type=MESH,
            ),
            pltpu.make_async_remote_copy(
                field.at[k, inner, pl.ds(4, 4)],
                y_halo.at[k, :, pl.ds(4, 4)],
                face_send.at[k, 1],
                face_recv.at[k, 1],
                device_id=(gx, y_next),
                device_id_type=MESH,
            ),
            pltpu.make_async_remote_copy(
                x_send.at[k],
                x_recv.at[k, 1],
                face_send.at[k, 2],
                face_recv.at[k, 2],
                device_id=(x_prev, gy),
                device_id_type=MESH,
            ),
            pltpu.make_async_remote_copy(
                x_send.at[k],
                x_recv.at[k, 0],
                face_send.at[k, 3],
                face_recv.at[k, 3],
                device_id=(x_next, gy),
                device_id_type=MESH,
            ),
        )

    def send_faces(k):
        for copy in face_copies(k):
            copy.start()

    def take_faces(k):
        for copy in face_copies(k):
            copy.wait_recv()

    y_inside = ((sub < 4) & (gy < rows - 1)) | ((sub >= 4) & (gy > 0))
    from_prev = lax.rem(lane, EDGE) < 4
    x_inside = (from_prev & (gx > 0)) | (jnp.logical_not(from_prev) & (gx < groups - 1))

    def unpack(k):
        for part in range(parts):
            both = jnp.where(from_prev, x_recv[k, 0, part], x_recv[k, 1, part])
            both = jnp.where(x_inside, both, 0.0)
            for i in range(per_part):
                x_halo[part * per_part + i] = pltpu.roll(both, (128 - EDGE * i - PAD) % 128, 1)

    def laplace(k, z):
        shape = (STEP_Z, 8, 128)
        lane3, sub3 = iota(shape, 2), iota(shape, 1)
        centre = field[k, pl.ds(z + PAD, STEP_Z)]
        over_y = jnp.where(y_inside[None], y_halo[k, pl.ds(z, STEP_Z)], 0.0)
        over_x = x_halo[pl.ds(z, STEP_Z)]
        total = (3.0 * STENCIL[0]) * centre
        for off in range(1, 5):
            near = field[k, pl.ds(z + PAD + off, STEP_Z)] + field[k, pl.ds(z + PAD - off, STEP_Z)]
            near += pltpu.roll(jnp.where(sub3 < off, over_y, centre), 8 - off, 1)
            near += pltpu.roll(jnp.where(sub3 >= 8 - off, over_y, centre), off, 1)
            near += pltpu.roll(jnp.where(lane3 < off, over_x, centre), 128 - off, 2)
            near += pltpu.roll(jnp.where(lane3 >= 128 - off, over_x, centre), off, 2)
            total += STENCIL[off] * near
        return total

    def box_copy(kind, d):
        to = lax.rem(gx + d, groups)
        return pltpu.make_async_remote_copy(
            out_box.at[kind, to // 2],
            in_box.at[kind, gx],
            box_send.at[kind, d],
            box_recv.at[kind, d],
            device_id=(to, gy),
            device_id_type=MESH,
        )

    def post(kind, top, bottom):
        for j in range(groups // 2):
            piece = slice(128 * j, 128 * j + 128)
            out_box[kind, j, 0:1] = top[:, piece]
            out_box[kind, j, 1:2] = bottom[:, piece]

        def start(d, carry):
            box_copy(kind, d).start()
            return carry

        lax.fori_loop(1, groups, start, 0)
        in_box[kind, gx] = out_box[kind, gx // 2]

    odd = lax.rem(gx, 2) == 1

    def collect(kind):
        def wait(d, carry):
            box_copy(kind, d).wait_recv()
            return carry

        lax.fori_loop(1, groups, wait, 0)
        first, second = [], []
        low = iota((2, 128), 1) < 64
        for j in range(groups // 2):
            a, b = in_box[kind, 2 * j], in_box[kind, 2 * j + 1]
            a = jnp.where(odd, pltpu.roll(a, 64, 1), a)
            b = jnp.where(odd, b, pltpu.roll(b, 64, 1))
            both = jnp.where(low, a, b)
            first.append(both[0:1])
            second.append(both[1:2])
        return jnp.concatenate(first, axis=1), jnp.concatenate(second, axis=1)

    def rows_of(top, bottom):
        width = top.shape[1]
        at = iota((8, width), 0)
        wide = jnp.where(
            at < 3, jnp.broadcast_to(top, (8, width)), jnp.broadcast_to(bottom, (8, width))
        )
        parts3 = [p.astype(F32) for p in split3(wide)]
        which = lax.rem(at, 3)
        chosen = jnp.where(which == 0, parts3[0], jnp.where(which == 1, parts3[1], parts3[2]))
        return jnp.where(at < 6, chosen, 0.0).astype(BF16)

    def sum_rows(out):
        return (out[0:1] + out[1:2]) + out[2:3], (out[3:4] + out[4:5]) + out[5:6]

    for k in range(4):
        field[k, 0:PAD] = jnp.zeros((PAD, 8, 128), F32)
        field[k, pl.ds(nz + PAD, PAD)] = jnp.zeros((PAD, 8, 128), F32)
    field[0, pl.ds(PAD, nz)] = wn_ref[...]
    pack(0)
    pl.semaphore_wait(barrier, groups + 1)
    send_faces(0)

    holder = hold_ref[...].astype(F32)
    row = (cell_ref[...] // 128).astype(F32)
    column = lax.rem(cell_ref[...], 128).astype(F32)
    at = iota((8, points), 0)
    facts = jnp.where(at == 0, holder, jnp.where(at == 1, row, column)).astype(BF16)
    source, place = iota((points, points), 0), iota((points, points), 1)
    half = points // 2
    order = jnp.where(place < half, 2 * place, 2 * (place - half) + 1)
    facts = nn(facts, jnp.where(source == order, 1.0, 0.0).astype(BF16))
    holder = facts[0:1]
    named = jnp.where(iota((groups, points), 0).astype(F32) == holder, 1.0, 0.0)
    before = nn(named.astype(BF16), jnp.where(source < place, 1.0, 0.0).astype(BF16))
    rank = jnp.sum(named * before, axis=0, keepdims=True)
    slot = holder * cap + rank
    for s in range(0, slots, 256):
        match[s : s + 256] = jnp.where(
            (iota((256, points), 0) + s).astype(F32) == slot, 1.0, 0.0
        ).astype(BF16)
    asked = nt(facts.astype(BF16), match[...])
    post(0, asked[1:2], asked[2:3])

    take_faces(0)
    unpack(0)

    def level_two(c, carry):
        z = c * STEP_Z
        here = pl.ds(z, STEP_Z)
        one = laplace(0, z)
        lap[0, here] = one
        field[1, pl.ds(z + PAD, STEP_Z)] = 2.0 * wn_ref[here] - wb_ref[here] + vt_ref[here] * one
        return carry

    lax.fori_loop(0, nz // STEP_Z, level_two, 0, unroll=True)
    pack(1)
    send_faces(1)

    row, column = collect(0)
    for s in range(0, slots, 256):
        piece = slice(s, s + 256)
        at_row[:, piece] = jnp.where(
            iota((nz * 8, 256), 0).astype(F32) == row[:, piece], 1.0, 0.0
        ).astype(BF16)
        at_lane[:, piece] = jnp.where(
            iota((128, 256), 0).astype(F32) == column[:, piece], 1.0, 0.0
        )

    def sample(values):
        turned = values.reshape(nz * 8, 128).T
        stacked = jnp.concatenate(split3(turned), axis=0)
        found = []
        for s in range(0, slots, 256):
            piece = slice(s, s + 256)
            got = nn(stacked, at_row[:, piece])
            got = (got[0:128] + got[128:256]) + got[256:384]
            found.append(jnp.sum(got * at_lane[:, piece], axis=0, keepdims=True))
        return jnp.concatenate(found, axis=1)

    sample_two = sample(field[1, pl.ds(PAD, nz)])

    take_faces(1)
    unpack(1)

    def level_three(c, carry):
        z = c * STEP_Z
        here = pl.ds(z, STEP_Z)
        two = laplace(1, z)
        lap[1, here] = two
        last[here] = 2.0 * field[1, pl.ds(z + PAD, STEP_Z)] - wn_ref[here] + vt_ref[here] * two
        return carry

    lax.fori_loop(0, nz // STEP_Z, level_three, 0, unroll=True)
    sample_last = sample(last[...])
    post(1, sample_two, sample_last)

    two, three = collect(1)
    two, three = sum_rows(nn(rows_of(two, three), match[...]))
    diff_two = two[:, half:] - two[:, :half]
    diff_last = three[:, half:] - three[:, :half]
    coupling = coup_ref[...]
    error_two = coupling * diff_two - obs_ref[0:1]
    error_last = coupling * diff_last - obs_ref[1:2]
    gc_ref[...] = error_two * diff_two + error_last * diff_last
    push_two = coupling * error_two
    push_last = coupling * error_last
    push = nt(
        rows_of(
            jnp.concatenate([-push_two, push_two], axis=1),
            jnp.concatenate([-push_last, push_last], axis=1),
        ),
        match[...],
    )
    post(2, *sum_rows(push))

    sources = collect(2)

    def inject(source):
        total = None
        for part in split3(source):
            spread = (at_lane[...] * part.astype(F32)).astype(BF16)
            got = nt(at_row[...], spread)
            total = got if total is None else total + got
        return total.reshape(nz, 8, 128)

    three = al_ref[...] + inject(sources[1])
    adj3[...] = three
    field[2, pl.ds(PAD, nz)] = vt_ref[...] * three
    pack(2)
    send_faces(2)
    am_ref[...] = an_ref[...] + inject(sources[0]) + 2.0 * adj3[...]
    take_faces(2)
    unpack(2)

    def adjoint_two(c, carry):
        z = c * STEP_Z
        here = pl.ds(z, STEP_Z)
        middle = am_ref[here] + laplace(2, z)
        am_ref[here] = middle
        field[3, pl.ds(z + PAD, STEP_Z)] = vt_ref[here] * middle
        return carry

    lax.fori_loop(0, nz // STEP_Z, adjoint_two, 0, unroll=True)
    pack(3)
    send_faces(3)
    gv_ref[...] = adj3[...] * lap[1] + am_ref[...] * lap[0]
    take_faces(3)
    unpack(3)

    def adjoint_one(c, carry):
        z = c * STEP_Z
        here = pl.ds(z, STEP_Z)
        ae_ref[here] = 2.0 * am_ref[here] - adj3[here] + laplace(3, z)
        return carry

    lax.fori_loop(0, nz // STEP_Z, adjoint_one, 0, unroll=True)

    for k in range(4):
        for copy in face_copies(k):
            copy.wait_send()

    def gone(d, carry):
        for kind in range(3):
            box_copy(kind, d).wait_send()
        return carry

    lax.fori_loop(1, groups, gone, 0)


def per_device(
    velocity_term,
    wave_before,
    wave_now,
    adjoint_later,
    adjoint_next,
    point_holder,
    point_cell,
    coupling,
    observed,
):
    nz, cy, cx = velocity_term.shape
    points = point_cell.shape[0]
    channels = coupling.shape[0]
    groups, rows = lax.axis_size("gx"), lax.axis_size("gy")
    slots = groups * 64
    parts = nz * EDGE // 128
    block = jax.ShapeDtypeStruct((nz, cy, cx), F32)
    vmem = pl.BlockSpec(memory_space=pltpu.VMEM)
    grad_velocity, grad_coupling, adjoint_early, adjoint_middle = pl.pallas_call(
        functools.partial(kernel, groups, rows),
        out_shape=(block, jax.ShapeDtypeStruct((1, channels), F32), block, block),
        in_specs=[vmem] * 9,
        out_specs=[vmem] * 4,
        scratch_shapes=[
            pltpu.VMEM((4, nz + 2 * PAD, cy, cx), F32),
            pltpu.VMEM((2, nz, cy, cx), F32),
            pltpu.VMEM((nz, cy, cx), F32),
            pltpu.VMEM((nz, cy, cx), F32),
            pltpu.VMEM((4, nz, cy, cx), F32),
            pltpu.VMEM((4, parts, cy, cx), F32),
            pltpu.VMEM((4, 2, parts, cy, cx), F32),
            pltpu.VMEM((nz, cy, cx), F32),
            pltpu.VMEM((slots, points), BF16),
            pltpu.VMEM((nz * cy, slots), BF16),
            pltpu.VMEM((cx, slots), F32),
            pltpu.VMEM((3, groups // 2, 2, 128), F32),
            pltpu.VMEM((3, groups, 2, 128), F32),
            pltpu.SemaphoreType.DMA((4, 4)),
            pltpu.SemaphoreType.DMA((4, 4)),
            pltpu.SemaphoreType.DMA((3, groups)),
            pltpu.SemaphoreType.DMA((3, groups)),
        ],
        compiler_params=pltpu.CompilerParams(
            collective_id=0, has_side_effects=True, vmem_limit_bytes=40 * 1024 * 1024
        ),
    )(
        velocity_term,
        wave_before,
        wave_now,
        adjoint_later,
        adjoint_next,
        point_holder.reshape(1, points),
        point_cell.reshape(1, points),
        coupling.reshape(1, channels),
        observed,
    )
    return grad_velocity, grad_coupling.reshape(channels), adjoint_early, adjoint_middle


def solution(mesh):
    grid = P(None, "gy", "gx")
    both = ("gx", "gy")
    return jax.shard_map(
        per_device,
        mesh=mesh,
        in_specs=(grid, grid, grid, grid, grid, P(both, None), P(both), P(both), P(None, both)),
        out_specs=(grid, P(both), grid, grid),
        check_vma=False,
    )
```

time: 266 us -> 56.4 us (0.21)
  the two profiles are of different devices: /device:TPU:6 before, /device:TPU:1 now
where the time goes in v1:
time: 56.4 us; the launch traced here: 55.3 us
  Pallas kernels  46.9 us (83%)
  local copies, waits for them, and re-layouts  7.68 us (14%)
  between operations  0.68 us (1%)
    pallas_call x1, Pallas kernels, per_device(): pl.pallas_call(functools.partial(kernel, groups, rows), out_shape=(block,...  46.9 us
    unnamed x22, local copies, waits for them, and re-layouts  7.68 us

profile of v1, /device:TPU:1, one launch (start us, length us, event | category | flops | bytes accessed | tf_op | source)
XLA Modules:
  0.0 55.3 jit_solution(15168163278282575287)
XLA Ops:
  0.6 0.0 copy-start.6
  0.6 0.0 copy-start.7
  0.7 0.0 copy-start.5
  0.7 0.0 copy-start.8
  0.7 0.6 %copy-done.6 = s32[256]{0:T(256)S(1)} copy-done((s32[256]{0:T(256)S(1)}, s32[256]{0:T(256)}, u32[]{:S(2)}) %copy-start.6) | copy-done | bytes 1048
  1.3 0.0 copy-done.7
  1.3 0.0 copy-done.5
  1.3 0.0 copy-done.8
  1.3 0.0 copy-start
  1.4 0.9 %copy-done = f32[32,8,128]{2,1,0:T(8,128)S(1)} copy-done((f32[32,8,128]{2,1,0:T(8,128)S(1)}, f32[32,8,128]{2,1,0:T(8,128)}, u32[]{:S(2)}) %copy-start) | copy-done | bytes 131096
  2.3 0.0 copy-start.1
  2.3 0.9 %copy-done.1 = f32[32,8,128]{2,1,0:T(8,128)S(1)} copy-done((f32[32,8,128]{2,1,0:T(8,128)S(1)}, f32[32,8,128]{2,1,0:T(8,128)}, u32[]{:S(2)}) %copy-start.1) | copy-done | bytes 131096
  3.2 0.0 copy-start.2
  3.2 0.9 %copy-done.2 = f32[32,8,128]{2,1,0:T(8,128)S(1)} copy-done((f32[32,8,128]{2,1,0:T(8,128)S(1)}, f32[32,8,128]{2,1,0:T(8,128)}, u32[]{:S(2)}) %copy-start.2) | copy-done | bytes 131096
  4.1 0.0 copy-start.3
  4.1 0.9 %copy-done.3 = f32[32,8,128]{2,1,0:T(8,128)S(1)} copy-done((f32[32,8,128]{2,1,0:T(8,128)S(1)}, f32[32,8,128]{2,1,0:T(8,128)}, u32[]{:S(2)}) %copy-start.3) | copy-done | bytes 131096
  5.0 0.0 copy-start.4
  5.0 0.9 %copy-done.4 = f32[32,8,128]{2,1,0:T(8,128)S(1)} copy-done((f32[32,8,128]{2,1,0:T(8,128)S(1)}, f32[32,8,128]{2,1,0:T(8,128)}, u32[]{:S(2)}) %copy-start.4) | copy-done | bytes 131096
  5.9 46.9 %shard_map.120 = (f32[32,8,128]{2,1,0:T(8,128)S(1)}, f32[1,128]{1,0:T(1,128)S(1)}, f32[32,8,128]{2,1,0:T(8,128)S(1)}, f32[32,8,128]{2,1,0:T(8,128)S(1)}) custom-call(f32[32,8,128]{2,1,0:T(8,128)S(1)} %copy-done, f32[32,8,128]{2,1,0:T(8,128)S(1)} %copy-done.1, f32[32,8,128]{2,1,0:T(8,128)S(1)} %copy-done.2, f32[32,8,128]{2,1,0:T(8,128)S(1)} %copy-done.3, ...), custom_call_target="tpu_custom_call" | custom-call | tf_op jit(solution)/shard_map/pallas_call | solution.py:414
  52.8 0.7 %copy.17 = f32[32,8,128]{2,1,0:T(8,128)} copy(f32[32,8,128]{2,1,0:T(8,128)S(1)} %get-tuple-element.16) | data formatting | bytes 262144
  53.4 0.5 copy.18
  54.0 0.7 %copy.19 = f32[32,8,128]{2,1,0:T(8,128)} copy(f32[32,8,128]{2,1,0:T(8,128)S(1)} %get-tuple-element.18) | data formatting | bytes 262144
  54.6 0.7 %copy.20 = f32[32,8,128]{2,1,0:T(8,128)} copy(f32[32,8,128]{2,1,0:T(8,128)S(1)} %get-tuple-element.19) | data formatting | bytes 262144
Async XLA Ops:
  0.6 0.7 %copy-start.6 = (s32[256]{0:T(256)S(1)}, s32[256]{0:T(256)}, u32[]{:S(2)}) copy-start(s32[256]{0:T(256)} %param.15) | copy-start | bytes 3076
  0.6 0.7 %copy-start.7 = (f32[2,128]{1,0:T(2,128)S(1)}, f32[2,128]{1,0:T(2,128)}, u32[]{:S(2)}) copy-start(f32[2,128]{1,0:T(2,128)} %obs_ref.1) | copy-start | bytes 3076
  0.7 0.7 %copy-start.5 = (s32[256,1]{0,1:T(1,128)S(1)}, s32[256,1]{0,1:T(1,128)}, u32[]{:S(2)}) copy-start(s32[256,1]{0,1:T(1,128)} %param.14) | copy-start | bytes 3076
  0.7 0.7 %copy-start.8 = (f32[128]{0:T(128)S(1)}, f32[128]{0:T(128)}, u32[]{:S(2)}) copy-start(f32[128]{0:T(128)} %param.16) | copy-start | bytes 1540
  1.3 0.9 %copy-start = (f32[32,8,128]{2,1,0:T(8,128)S(1)}, f32[32,8,128]{2,1,0:T(8,128)}, u32[]{:S(2)}) copy-start(f32[32,8,128]{2,1,0:T(8,128)} %vt_ref.1) | copy-start | bytes 393220
  2.3 0.9 %copy-start.1 = (f32[32,8,128]{2,1,0:T(8,128)S(1)}, f32[32,8,128]{2,1,0:T(8,128)}, u32[]{:S(2)}) copy-start(f32[32,8,128]{2,1,0:T(8,128)} %wb_ref.1) | copy-start | bytes 393220
  3.2 0.9 %copy-start.2 = (f32[32,8,128]{2,1,0:T(8,128)S(1)}, f32[32,8,128]{2,1,0:T(8,128)}, u32[]{:S(2)}) copy-start(f32[32,8,128]{2,1,0:T(8,128)} %wn_ref.1) | copy-start | bytes 393220
  4.1 0.9 %copy-start.3 = (f32[32,8,128]{2,1,0:T(8,128)S(1)}, f32[32,8,128]{2,1,0:T(8,128)}, u32[]{:S(2)}) copy-start(f32[32,8,128]{2,1,0:T(8,128)} %al_ref.1) | copy-start | bytes 393220
  5.0 0.9 %copy-start.4 = (f32[32,8,128]{2,1,0:T(8,128)S(1)}, f32[32,8,128]{2,1,0:T(8,128)}, u32[]{:S(2)}) copy-start(f32[32,8,128]{2,1,0:T(8,128)} %an_ref.1) | copy-start | bytes 393220

commit v2 on v1

--- a/solution.py
+++ b/solution.py
@@ -39,19 +39,27 @@
 def kernel(
     groups,
     rows,
+    vt_hbm,
+    wb_hbm,
+    wn_hbm,
+    al_hbm,
+    an_hbm,
+    hold_hbm,
+    cell_hbm,
+    coup_hbm,
+    obs_hbm,
+    gv_ref,
+    gc_ref,
+    ae_ref,
+    am_ref,
     vt_ref,
     wb_ref,
-    wn_ref,
     al_ref,
     an_ref,
     hold_ref,
     cell_ref,
     coup_ref,
     obs_ref,
-    gv_ref,
-    gc_ref,
-    ae_ref,
-    am_ref,
     field,
     lap,
     last,
@@ -69,6 +77,7 @@
     face_recv,
     box_send,
     box_recv,
+    load_sem,
 ):
     nz = vt_ref.shape[0]
     per_part = 128 // EDGE
@@ -80,6 +89,26 @@
     gy = lax.axis_index("gy")
     x_prev, x_next = lax.rem(gx + groups - 1, groups), lax.rem(gx + 1, groups)
     y_prev, y_next = lax.rem(gy + rows - 1, rows), lax.rem(gy + 1, rows)
+
+    wn_ref = field.at[0, pl.ds(PAD, nz)]
+    loads = [
+        pltpu.make_async_copy(far, near, load_sem.at[i])
+        for i, (far, near) in enumerate(
+            (
+                (wn_hbm, wn_ref),
+                (hold_hbm, hold_ref),
+                (cell_hbm, cell_ref),
+                (vt_hbm, vt_ref),
+                (wb_hbm, wb_ref),
+                (coup_hbm, coup_ref),
+                (obs_hbm, obs_ref),
+                (al_hbm, al_ref),
+                (an_hbm, an_ref),
+            )
+        )
+    ]
+    for copy in loads:
+        copy.start()
 
     barrier = pltpu.get_barrier_semaphore()
 
@@ -148,6 +177,7 @@
     def send_faces(k):
         for copy in face_copies(k):
             copy.start()
+        faces_out.append(k)
 
     def take_faces(k):
         for copy in face_copies(k):
@@ -180,6 +210,10 @@
             total += STENCIL[off] * near
         return total
 
+    def far_first(d):
+        step = d % 8
+        return -min(step, 8 - step), d
+
     def box_copy(kind, d):
         to = lax.rem(gx + d, groups)
         return pltpu.make_async_remote_copy(
@@ -191,17 +225,16 @@
             device_id_type=MESH,
         )
 
-    def post(kind, top, bottom):
+    def fill(kind, top, bottom):
         for j in range(groups // 2):
             piece = slice(128 * j, 128 * j + 128)
             out_box[kind, j, 0:1] = top[:, piece]
             out_box[kind, j, 1:2] = bottom[:, piece]
 
-        def start(d, carry):
+    def post(kind):
+        for d in sorted(range(1, groups), key=far_first):
             box_copy(kind, d).start()
-            return carry
-
-        lax.fori_loop(1, groups, start, 0)
+        boxes_out.append(kind)
         in_box[kind, gx] = out_box[kind, gx // 2]
 
     odd = lax.rem(gx, 2) == 1
@@ -237,13 +270,25 @@
     def sum_rows(out):
         return (out[0:1] + out[1:2]) + out[2:3], (out[3:4] + out[4:5]) + out[5:6]
 
+    faces_out, boxes_out = [], []
+
+    def finish():
+        for k in faces_out:
+            for copy in face_copies(k):
+                copy.wait_send()
+
+        def gone(d, carry):
+            for kind in boxes_out:
+                box_copy(kind, d).wait_send()
+            return carry
+
+        lax.fori_loop(1, groups, gone, 0)
+
     for k in range(4):
         field[k, 0:PAD] = jnp.zeros((PAD, 8, 128), F32)
         field[k, pl.ds(nz + PAD, PAD)] = jnp.zeros((PAD, 8, 128), F32)
-    field[0, pl.ds(PAD, nz)] = wn_ref[...]
-    pack(0)
-    pl.semaphore_wait(barrier, groups + 1)
-    send_faces(0)
+    for copy in loads[1:3]:
+        copy.wait()
 
     holder = hold_ref[...].astype(F32)
     row = (cell_ref[...] // 128).astype(F32)
@@ -264,8 +309,15 @@
             (iota((256, points), 0) + s).astype(F32) == slot, 1.0, 0.0
         ).astype(BF16)
     asked = nt(facts.astype(BF16), match[...])
-    post(0, asked[1:2], asked[2:3])
-
+    fill(0, asked[1:2], asked[2:3])
+    loads[0].wait()
+    pack(0)
+    pl.semaphore_wait(barrier, groups + 1)
+    send_faces(0)
+    post(0)
+
+    for copy in loads[3:5]:
+        copy.wait()
     take_faces(0)
     unpack(0)
 
@@ -274,7 +326,7 @@
         here = pl.ds(z, STEP_Z)
         one = laplace(0, z)
         lap[0, here] = one
-        field[1, pl.ds(z + PAD, STEP_Z)] = 2.0 * wn_ref[here] - wb_ref[here] + vt_ref[here] * one
+        field[1, pl.ds(z + PAD, STEP_Z)] = 2.0 * field[0, pl.ds(z + PAD, STEP_Z)] - wb_ref[here] + vt_ref[here] * one
         return carry
 
     lax.fori_loop(0, nz // STEP_Z, level_two, 0, unroll=True)
@@ -312,14 +364,17 @@
         here = pl.ds(z, STEP_Z)
         two = laplace(1, z)
         lap[1, here] = two
-        last[here] = 2.0 * field[1, pl.ds(z + PAD, STEP_Z)] - wn_ref[here] + vt_ref[here] * two
+        last[here] = 2.0 * field[1, pl.ds(z + PAD, STEP_Z)] - field[0, pl.ds(z + PAD, STEP_Z)] + vt_ref[here] * two
         return carry
 
     lax.fori_loop(0, nz // STEP_Z, level_three, 0, unroll=True)
     sample_last = sample(last[...])
-    post(1, sample_two, sample_last)
+    fill(1, sample_two, sample_last)
+    post(1)
 
     two, three = collect(1)
+    for copy in loads[5:]:
+        copy.wait()
     two, three = sum_rows(nn(rows_of(two, three), match[...]))
     diff_two = two[:, half:] - two[:, :half]
     diff_last = three[:, half:] - three[:, :half]
@@ -336,7 +391,8 @@
         ),
         match[...],
     )
-    post(2, *sum_rows(push))
+    fill(2, *sum_rows(push))
+    post(2)
 
     sources = collect(2)
 
@@ -380,16 +436,16 @@
 
     lax.fori_loop(0, nz // STEP_Z, adjoint_one, 0, unroll=True)
 
-    for k in range(4):
-        for copy in face_copies(k):
-            copy.wait_send()
-
-    def gone(d, carry):
-        for kind in range(3):
-            box_copy(kind, d).wait_send()
-        return carry
-
-    lax.fori_loop(1, groups, gone, 0)
+    finish()
+
+
+def write_kernel(*refs):
+    near, far, sem = refs[:4], refs[4:8], refs[8]
+    copies = [pltpu.make_async_copy(near[i], far[i], sem.at[i]) for i in range(4)]
+    for copy in copies:
+        copy.start()
+    for copy in copies:
+        copy.wait()
 
 
 def per_device(
@@ -411,12 +467,23 @@
     parts = nz * EDGE // 128
     block = jax.ShapeDtypeStruct((nz, cy, cx), F32)
     vmem = pl.BlockSpec(memory_space=pltpu.VMEM)
-    grad_velocity, grad_coupling, adjoint_early, adjoint_middle = pl.pallas_call(
+    hbm = pl.BlockSpec(memory_space=pltpu.HBM)
+    found = (block, jax.ShapeDtypeStruct((1, channels), F32), block, block)
+    close = tuple(pltpu.VMEM(leaf.shape, leaf.dtype) for leaf in found)
+    near = pl.pallas_call(
         functools.partial(kernel, groups, rows),
-        out_shape=(block, jax.ShapeDtypeStruct((1, channels), F32), block, block),
-        in_specs=[vmem] * 9,
+        out_shape=close,
+        in_specs=[hbm] * 9,
         out_specs=[vmem] * 4,
         scratch_shapes=[
+            pltpu.VMEM((nz, cy, cx), F32),
+            pltpu.VMEM((nz, cy, cx), F32),
+            pltpu.VMEM((nz, cy, cx), F32),
+            pltpu.VMEM((nz, cy, cx), F32),
+            pltpu.VMEM((1, points), jnp.int32),
+            pltpu.VMEM((1, points), jnp.int32),
+            pltpu.VMEM((1, channels), F32),
+            pltpu.VMEM((2, channels), F32),
             pltpu.VMEM((4, nz + 2 * PAD, cy, cx), F32),
             pltpu.VMEM((2, nz, cy, cx), F32),
             pltpu.VMEM((nz, cy, cx), F32),
@@ -434,21 +501,34 @@
             pltpu.SemaphoreType.DMA((4, 4)),
             pltpu.SemaphoreType.DMA((3, groups)),
             pltpu.SemaphoreType.DMA((3, groups)),
+            pltpu.SemaphoreType.DMA((9,)),
         ],
         compiler_params=pltpu.CompilerParams(
             collective_id=0, has_side_effects=True, vmem_limit_bytes=40 * 1024 * 1024
         ),
     )(
-        velocity_term,
-        wave_before,
-        wave_now,
-        adjoint_later,
-        adjoint_next,
-        point_holder.reshape(1, points),
-        point_cell.reshape(1, points),
-        coupling.reshape(1, channels),
-        observed,
+        *(
+            pltpu.with_memory_space_constraint(x, pltpu.HBM)
+            for x in (
+                velocity_term,
+                wave_before,
+                wave_now,
+                adjoint_later,
+                adjoint_next,
+                point_holder.reshape(1, points),
+                point_cell.reshape(1, points),
+                coupling.reshape(1, channels),
+                observed,
+            )
+        )
     )
+    grad_velocity, grad_coupling, adjoint_early, adjoint_middle = pl.pallas_call(
+        write_kernel,
+        out_shape=found,
+        in_specs=[vmem] * 4,
+        out_specs=[hbm] * 4,
+        scratch_shapes=[pltpu.SemaphoreType.DMA((4,))],
+    )(*(pltpu.with_memory_space_constraint(x, pltpu.VMEM) for x in near))
     return grad_velocity, grad_coupling.reshape(channels), adjoint_early, adjoint_middle
 
 

time: 56.4 us -> 49.2 us (0.87)
  local copies, waits for them, and re-layouts: 7.68 us -> 0 us
  Pallas kernels: 46.9 us -> 47.6 us
    unnamed x22 -> x0, local copies, waits for them, and re-layouts: 7.68 us -> none
    pallas_call x1 -> x2, Pallas kernels: 46.9 us -> 47.6 us  [the longest x1 46.8 us: per_device(): pl.pallas_call(functools.partial(kernel, groups, rows), out_shape=close,...]
where the time goes in v2:
time: 49.2 us; the launch traced here: 48.2 us
  Pallas kernels  47.6 us (97%)
  between operations  0.64 us (1%)
    pallas_call x1, Pallas kernels, per_device(): pl.pallas_call(functools.partial(kernel, groups, rows), out_shape=close,...  46.8 us

profile of v2, /device:TPU:1, one launch (start us, length us, event | category | flops | bytes accessed | tf_op | source)
XLA Modules:
  0.0 48.2 jit_solution(1115601911793206700)
XLA Ops:
  0.6 46.8 %shard_map.120 = (f32[32,8,128]{2,1,0:T(8,128)S(1)}, f32[1,128]{1,0:T(1,128)S(1)}, f32[32,8,128]{2,1,0:T(8,128)S(1)}, f32[32,8,128]{2,1,0:T(8,128)S(1)}) custom-call(f32[32,8,128]{2,1,0:T(8,128)} %vt_hbm.1, f32[32,8,128]{2,1,0:T(8,128)} %wb_hbm.1, f32[32,8,128]{2,1,0:T(8,128)} %wn_hbm.1, f32[32,8,128]{2,1,0:T(8,128)} %al_hbm.1, f32[32,8,128]{2,1,0:T(8,128)} %an_hbm.1, ...), custom_call_target="tpu_custom_call" | custom-call | tf_op jit(solution)/shard_map/pallas_call | solution.py:473
  47.5 0.8 %shard_map.121 = (f32[32,8,128]{2,1,0:T(8,128)}, f32[1,128]{1,0:T(1,128)}, f32[32,8,128]{2,1,0:T(8,128)}, f32[32,8,128]{2,1,0:T(8,128)}) custom-call(f32[32,8,128]{2,1,0:T(8,128)S(1)} %get-tuple-element.12.refs_0_, f32[1,128]{1,0:T(1,128)S(1)} %get-tuple-element.13.refs_1_, f32[32,8,128]{2,1,0:T(8,128)S(1)} %get-tuple-element.14.refs_2_, ...), custom_call_target="tpu_custom_call" | custom-call | tf_op jit(solution)/shard_map/pallas_call | solution.py:525

commit v3 on v2

--- a/solution.py
+++ b/solution.py
@@ -13,7 +13,8 @@
 BF16 = jnp.bfloat16
 PAD = 4
 STEP_Z = 4
-EDGE = 8
+MAIN = 16
+SIDE = 8
 
 
 def iota(shape, dim):
@@ -61,13 +62,18 @@
     coup_ref,
     obs_ref,
     field,
+    strip_y,
+    strip_x,
+    far_y,
+    corner,
+    side_y,
+    side_x,
     lap,
     last,
+    known,
     adj3,
-    y_halo,
     x_send,
     x_recv,
-    x_halo,
     match,
     at_row,
     at_lane,
@@ -80,8 +86,7 @@
     load_sem,
 ):
     nz = vt_ref.shape[0]
-    per_part = 128 // EDGE
-    parts = x_send.shape[1]
+    main_parts, side_parts = nz * MAIN // 128, nz * SIDE // 128
     cap = 64
     slots = groups * cap
     points = hold_ref.shape[1]
@@ -122,93 +127,196 @@
     for other in (y_prev, y_next):
         pl.semaphore_signal(barrier, inc=1, device_id=(gx, other), device_id_type=MESH)
 
+    for x in (x_prev, x_next):
+        for y in (y_prev, y_next):
+            pl.semaphore_signal(barrier, inc=1, device_id=(x, y), device_id_type=MESH)
+
     lane = iota((8, 128), 1)
     sub = iota((8, 128), 0)
 
-    def pack(k):
-        for part in range(parts):
+    def pack(e, at, width, read):
+        per_part = 128 // width
+        for part in range(nz // per_part):
             packed = None
             for i in range(per_part):
-                turned = pltpu.roll(
-                    field[k, PAD + part * per_part + i], (EDGE * i + PAD) % 128, 1
-                )
-                packed = (
-                    turned if packed is None else jnp.where(lane // EDGE == i, turned, packed)
-                )
-            x_send[k, part] = packed
-
-    def face_copies(k):
-        inner = pl.ds(PAD, nz)
-        return (
-            pltpu.make_async_remote_copy(
-                field.at[k, inner, pl.ds(0, 4)],
-                y_halo.at[k, :, pl.ds(0, 4)],
-                face_send.at[k, 0],
-                face_recv.at[k, 0],
-                device_id=(gx, y_prev),
-                device_id_type=MESH,
-            ),
-            pltpu.make_async_remote_copy(
-                field.at[k, inner, pl.ds(4, 4)],
-                y_halo.at[k, :, pl.ds(4, 4)],
-                face_send.at[k, 1],
-                face_recv.at[k, 1],
-                device_id=(gx, y_next),
-                device_id_type=MESH,
-            ),
-            pltpu.make_async_remote_copy(
-                x_send.at[k],
-                x_recv.at[k, 1],
-                face_send.at[k, 2],
-                face_recv.at[k, 2],
-                device_id=(x_prev, gy),
-                device_id_type=MESH,
-            ),
-            pltpu.make_async_remote_copy(
-                x_send.at[k],
-                x_recv.at[k, 0],
-                face_send.at[k, 3],
-                face_recv.at[k, 3],
-                device_id=(x_next, gy),
-                device_id_type=MESH,
-            ),
-        )
-
-    def send_faces(k):
-        for copy in face_copies(k):
+                turned = pltpu.roll(read(part * per_part + i), (width * i + width // 2) % 128, 1)
+                packed = turned if packed is None else jnp.where(lane // width == i, turned, packed)
+            x_send[e, at + part] = packed
+
+    def unpack(width, parts, write):
+        per_part = 128 // width
+        for part, both in enumerate(parts):
+            for i in range(per_part):
+                write(part * per_part + i, pltpu.roll(both, (256 - width * i - width // 2) % 128, 1))
+
+    def remote(source, target, e, i, device):
+        return pltpu.make_async_remote_copy(
+            source,
+            target,
+            face_send.at[e, i],
+            face_recv.at[e, i],
+            device_id=device,
+            device_id_type=MESH,
+        )
+
+    low, high, inner = pl.ds(0, 4), pl.ds(4, 4), pl.ds(PAD, nz)
+    mains = (wn_hbm, field.at[2, inner])
+    sides = (((vt_hbm, 0), (wb_hbm, 1)), ((known, 2),))
+    below, above = (gx, y_prev), (gx, y_next)
+
+    def rows_main(e):
+        near, far = strip_y.at[2 * e, inner], far_y.at[e]
+        return [
+            remote(mains[e].at[:, low], near.at[:, low], e, 0, below),
+            remote(mains[e].at[:, high], near.at[:, high], e, 1, above),
+            remote(mains[e].at[:, high], far.at[:, high], e, 2, below),
+            remote(mains[e].at[:, low], far.at[:, low], e, 3, above),
+        ]
+
+    def rows_side(e):
+        copies = []
+        for i, (source, kept) in enumerate(sides[e]):
+            target = side_y.at[kept]
+            copies += [
+                remote(source.at[:, low], target.at[:, low], e, 4 + 2 * i, below),
+                remote(source.at[:, high], target.at[:, high], e, 5 + 2 * i, above),
+            ]
+        return copies
+
+    def columns_main(e):
+        part = pl.ds(0, main_parts)
+        to = ((x_next, gy), (x_prev, gy), (x_next, y_next), (x_next, y_prev), (x_prev, y_next), (x_prev, y_prev))
+        return [remote(x_send.at[e, part], x_recv.at[e, i, part], e, 8 + i, to[i]) for i in (2, 3, 4, 5, 0, 1)]
+
+    def columns_side(e):
+        part = pl.ds(main_parts, side_parts * len(sides[e]))
+        to = ((x_next, gy), (x_prev, gy))
+        return [remote(x_send.at[e, part], x_recv.at[e, i, part], e, 14 + i, to[i]) for i in (0, 1)]
+
+    def send(kind, e):
+        for copy in kind(e):
             copy.start()
-        faces_out.append(k)
-
-    def take_faces(k):
-        for copy in face_copies(k):
+        faces_out.append((kind, e))
+
+    def take(kind, e):
+        for copy in kind(e):
             copy.wait_recv()
 
     y_inside = ((sub < 4) & (gy < rows - 1)) | ((sub >= 4) & (gy > 0))
-    from_prev = lax.rem(lane, EDGE) < 4
-    x_inside = (from_prev & (gx > 0)) | (jnp.logical_not(from_prev) & (gx < groups - 1))
-
-    def unpack(k):
-        for part in range(parts):
-            both = jnp.where(from_prev, x_recv[k, 0, part], x_recv[k, 1, part])
-            both = jnp.where(x_inside, both, 0.0)
-            for i in range(per_part):
-                x_halo[part * per_part + i] = pltpu.roll(both, (128 - EDGE * i - PAD) % 128, 1)
-
-    def laplace(k, z):
-        shape = (STEP_Z, 8, 128)
-        lane3, sub3 = iota(shape, 2), iota(shape, 1)
-        centre = field[k, pl.ds(z + PAD, STEP_Z)]
-        over_y = jnp.where(y_inside[None], y_halo[k, pl.ds(z, STEP_Z)], 0.0)
-        over_x = x_halo[pl.ds(z, STEP_Z)]
-        total = (3.0 * STENCIL[0]) * centre
+    x_inside = ((lane >= 64) & (gx > 0)) | ((lane < 64) & (gx < groups - 1))
+
+    def take_main(e):
+        take(rows_main, e)
+
+        @pl.when(gy == 0)
+        def _():
+            strip_y[2 * e, inner, high] = jnp.zeros((nz, 4, 128), F32)
+            far_y[e, :, low] = jnp.zeros((nz, 4, 128), F32)
+
+        @pl.when(gy == rows - 1)
+        def _():
+            strip_y[2 * e, inner, low] = jnp.zeros((nz, 4, 128), F32)
+            far_y[e, :, high] = jnp.zeros((nz, 4, 128), F32)
+
+        take(columns_main, e)
+        left = lax.rem(lane, MAIN) < MAIN // 2
+        exists = (left & (gx > 0)) | (jnp.logical_not(left) & (gx < groups - 1))
+        straight, across = [], []
+        for part in range(main_parts):
+            got = [x_recv[e, i, part] for i in range(6)]
+            straight.append(jnp.where(exists, jnp.where(left, got[0], got[1]), 0.0))
+            diagonal = jnp.where(
+                left, jnp.where(sub < 4, got[3], got[2]), jnp.where(sub < 4, got[5], got[4])
+            )
+            across.append(jnp.where(exists & y_inside, diagonal, 0.0))
+
+        def to_strip(z, value):
+            strip_x[2 * e, PAD + z] = value
+
+        def to_corner(z, value):
+            corner[e, z] = value
+
+        unpack(MAIN, straight, to_strip)
+        unpack(MAIN, across, to_corner)
+
+    def take_sides(e):
+        take(rows_side, e)
+        take(columns_side, e)
+        left = lax.rem(lane, SIDE) < SIDE // 2
+        for i, (_, kept) in enumerate(sides[e]):
+            first = main_parts + i * side_parts
+
+            def to_side(z, value, kept=kept):
+                side_x[kept, z] = value
+
+            unpack(
+                SIDE,
+                [jnp.where(left, x_recv[e, 0, first + p], x_recv[e, 1, first + p]) for p in range(side_parts)],
+                to_side,
+            )
+
+    def levels(buffer, k, z, off):
+        return buffer[k, pl.ds(z + PAD + off, STEP_Z)]
+
+    shape3 = (STEP_Z, 8, 128)
+    lane3, sub3 = iota(shape3, 2), iota(shape3, 1)
+
+    def cross(buffer, k, z, up, down, right, left):
+        total = (3.0 * STENCIL[0]) * levels(buffer, k, z, 0)
         for off in range(1, 5):
-            near = field[k, pl.ds(z + PAD + off, STEP_Z)] + field[k, pl.ds(z + PAD - off, STEP_Z)]
-            near += pltpu.roll(jnp.where(sub3 < off, over_y, centre), 8 - off, 1)
-            near += pltpu.roll(jnp.where(sub3 >= 8 - off, over_y, centre), off, 1)
-            near += pltpu.roll(jnp.where(lane3 < off, over_x, centre), 128 - off, 2)
-            near += pltpu.roll(jnp.where(lane3 >= 128 - off, over_x, centre), off, 2)
+            near = levels(buffer, k, z, off) + levels(buffer, k, z, -off)
+            near += pltpu.roll(up(off), 8 - off, 1) + pltpu.roll(down(off), off, 1)
+            near += pltpu.roll(right(off), 128 - off, 2) + pltpu.roll(left(off), off, 2)
             total += STENCIL[off] * near
         return total
+
+    def across_x(inside, outside):
+        return (
+            lambda off: jnp.where(lane3 < off, outside, inside),
+            lambda off: jnp.where(lane3 >= 128 - off, outside, inside),
+        )
+
+    def across_y(inside, outside):
+        return (
+            lambda off: jnp.where(sub3 < off, outside, inside),
+            lambda off: jnp.where(sub3 >= 8 - off, outside, inside),
+        )
+
+    def on_block(k, z):
+        own = levels(field, k, z, 0)
+        return cross(
+            field,
+            k,
+            z,
+            *across_y(own, levels(strip_y, k, z, 0)),
+            *across_x(own, levels(strip_x, k, z, 0)),
+        )
+
+    def on_strip_x(k, z):
+        own, strip = levels(field, k, z, 0), levels(strip_x, k, z, 0)
+        return cross(
+            strip_x,
+            k,
+            z,
+            *across_y(strip, corner[k // 2, pl.ds(z, STEP_Z)]),
+            *across_x(strip, own),
+        )
+
+    def on_strip_y(k, z):
+        own, strip = levels(field, k, z, 0), levels(strip_y, k, z, 0)
+        far = far_y[k // 2, pl.ds(z, STEP_Z)]
+
+        def up(off):
+            outer = jnp.where((sub3 >= 4) & (sub3 < 4 + off), far, strip)
+            return jnp.where(sub3 < off, own, outer)
+
+        def down(off):
+            outer = jnp.where((sub3 < 4) & (sub3 >= 4 - off), far, strip)
+            return jnp.where(sub3 >= 8 - off, own, outer)
+
+        return cross(
+            strip_y, k, z, up, down, *across_x(strip, corner[k // 2, pl.ds(z, STEP_Z)])
+        )
 
     def far_first(d):
         step = d % 8
@@ -273,8 +381,8 @@
     faces_out, boxes_out = [], []
 
     def finish():
-        for k in faces_out:
-            for copy in face_copies(k):
+        for kind, e in faces_out:
+            for copy in kind(e):
                 copy.wait_send()
 
         def gone(d, carry):
@@ -284,9 +392,21 @@
 
         lax.fori_loop(1, groups, gone, 0)
 
-    for k in range(4):
-        field[k, 0:PAD] = jnp.zeros((PAD, 8, 128), F32)
-        field[k, pl.ds(nz + PAD, PAD)] = jnp.zeros((PAD, 8, 128), F32)
+    pl.semaphore_wait(barrier, groups + 5)
+    send(rows_main, 0)
+    send(rows_side, 0)
+    for buffer, used in ((field, range(4)), (strip_y, (0, 2)), (strip_x, (0, 2))):
+        for k in used:
+            buffer[k, 0:PAD] = jnp.zeros((PAD, 8, 128), F32)
+            buffer[k, pl.ds(nz + PAD, PAD)] = jnp.zeros((PAD, 8, 128), F32)
+    loads[0].wait()
+    pack(0, 0, MAIN, lambda z: field[0, PAD + z])
+    send(columns_main, 0)
+    for copy in loads[3:5]:
+        copy.wait()
+    pack(0, main_parts, SIDE, lambda z: vt_ref[z])
+    pack(0, main_parts + side_parts, SIDE, lambda z: wb_ref[z])
+    send(columns_side, 0)
     for copy in loads[1:3]:
         copy.wait()
 
@@ -310,28 +430,36 @@
         ).astype(BF16)
     asked = nt(facts.astype(BF16), match[...])
     fill(0, asked[1:2], asked[2:3])
-    loads[0].wait()
-    pack(0)
-    pl.semaphore_wait(barrier, groups + 1)
-    send_faces(0)
     post(0)
 
-    for copy in loads[3:5]:
-        copy.wait()
-    take_faces(0)
-    unpack(0)
+    take_main(0)
+    take_sides(0)
 
     def level_two(c, carry):
         z = c * STEP_Z
         here = pl.ds(z, STEP_Z)
-        one = laplace(0, z)
+        put = pl.ds(z + PAD, STEP_Z)
+        one = on_block(0, z)
         lap[0, here] = one
-        field[1, pl.ds(z + PAD, STEP_Z)] = 2.0 * field[0, pl.ds(z + PAD, STEP_Z)] - wb_ref[here] + vt_ref[here] * one
+        field[1, put] = 2.0 * field[0, put] - wb_ref[here] + vt_ref[here] * one
+        value = 2.0 * strip_y[0, put] - side_y[1, here] + side_y[0, here] * on_strip_y(0, z)
+        strip_y[1, put] = jnp.where(y_inside[None], value, 0.0)
+        value = 2.0 * strip_x[0, put] - side_x[1, here] + side_x[0, here] * on_strip_x(0, z)
+        strip_x[1, put] = jnp.where(x_inside[None], value, 0.0)
         return carry
 
     lax.fori_loop(0, nz // STEP_Z, level_two, 0, unroll=True)
-    pack(1)
-    send_faces(1)
+
+    def level_three(c, carry):
+        z = c * STEP_Z
+        here = pl.ds(z, STEP_Z)
+        put = pl.ds(z + PAD, STEP_Z)
+        two = on_block(1, z)
+        lap[1, here] = two
+        last[here] = 2.0 * field[1, put] - field[0, put] + vt_ref[here] * two
+        return carry
+
+    lax.fori_loop(0, nz // STEP_Z, level_three, 0, unroll=True)
 
     row, column = collect(0)
     for s in range(0, slots, 256):
@@ -356,18 +484,6 @@
 
     sample_two = sample(field[1, pl.ds(PAD, nz)])
 
-    take_faces(1)
-    unpack(1)
-
-    def level_three(c, carry):
-        z = c * STEP_Z
-        here = pl.ds(z, STEP_Z)
-        two = laplace(1, z)
-        lap[1, here] = two
-        last[here] = 2.0 * field[1, pl.ds(z + PAD, STEP_Z)] - field[0, pl.ds(z + PAD, STEP_Z)] + vt_ref[here] * two
-        return carry
-
-    lax.fori_loop(0, nz // STEP_Z, level_three, 0, unroll=True)
     sample_last = sample(last[...])
     fill(1, sample_two, sample_last)
     post(1)
@@ -406,36 +522,40 @@
 
     three = al_ref[...] + inject(sources[1])
     adj3[...] = three
-    field[2, pl.ds(PAD, nz)] = vt_ref[...] * three
-    pack(2)
-    send_faces(2)
-    am_ref[...] = an_ref[...] + inject(sources[0]) + 2.0 * adj3[...]
-    take_faces(2)
-    unpack(2)
+    field[2, inner] = vt_ref[...] * three
+    send(rows_main, 1)
+    pack(1, 0, MAIN, lambda z: field[2, PAD + z])
+    send(columns_main, 1)
+    known[...] = an_ref[...] + inject(sources[0]) + 2.0 * adj3[...]
+    send(rows_side, 1)
+    pack(1, main_parts, SIDE, lambda z: known[z])
+    send(columns_side, 1)
+    take_main(1)
+    take_sides(1)
 
     def adjoint_two(c, carry):
         z = c * STEP_Z
         here = pl.ds(z, STEP_Z)
-        middle = am_ref[here] + laplace(2, z)
+        put = pl.ds(z + PAD, STEP_Z)
+        middle = known[here] + on_block(2, z)
         am_ref[here] = middle
-        field[3, pl.ds(z + PAD, STEP_Z)] = vt_ref[here] * middle
+        field[3, put] = vt_ref[here] * middle
+        value = side_y[0, here] * (side_y[2, here] + on_strip_y(2, z))
+        strip_y[3, put] = jnp.where(y_inside[None], value, 0.0)
+        value = side_x[0, here] * (side_x[2, here] + on_strip_x(2, z))
+        strip_x[3, put] = jnp.where(x_inside[None], value, 0.0)
+        gv_ref[here] = adj3[here] * lap[1, here] + middle * lap[0, here]
         return carry
 
     lax.fori_loop(0, nz // STEP_Z, adjoint_two, 0, unroll=True)
-    pack(3)
-    send_faces(3)
-    gv_ref[...] = adj3[...] * lap[1] + am_ref[...] * lap[0]
-    take_faces(3)
-    unpack(3)
 
     def adjoint_one(c, carry):
         z = c * STEP_Z
         here = pl.ds(z, STEP_Z)
-        ae_ref[here] = 2.0 * am_ref[here] - adj3[here] + laplace(3, z)
+        ae_ref[here] = 2.0 * am_ref[here] - adj3[here] + on_block(3, z)
         return carry
 
     lax.fori_loop(0, nz // STEP_Z, adjoint_one, 0, unroll=True)
-
     finish()
 
 
@@ -464,7 +584,7 @@
     channels = coupling.shape[0]
     groups, rows = lax.axis_size("gx"), lax.axis_size("gy")
     slots = groups * 64
-    parts = nz * EDGE // 128
+    parts = nz * (MAIN + 2 * SIDE) // 128
     block = jax.ShapeDtypeStruct((nz, cy, cx), F32)
     vmem = pl.BlockSpec(memory_space=pltpu.VMEM)
     hbm = pl.BlockSpec(memory_space=pltpu.HBM)
@@ -485,20 +605,25 @@
             pltpu.VMEM((1, channels), F32),
             pltpu.VMEM((2, channels), F32),
             pltpu.VMEM((4, nz + 2 * PAD, cy, cx), F32),
+            pltpu.VMEM((4, nz + 2 * PAD, cy, cx), F32),
+            pltpu.VMEM((4, nz + 2 * PAD, cy, cx), F32),
+            pltpu.VMEM((2, nz, cy, cx), F32),
+            pltpu.VMEM((2, nz, cy, cx), F32),
+            pltpu.VMEM((3, nz, cy, cx), F32),
+            pltpu.VMEM((3, nz, cy, cx), F32),
             pltpu.VMEM((2, nz, cy, cx), F32),
             pltpu.VMEM((nz, cy, cx), F32),
             pltpu.VMEM((nz, cy, cx), F32),
-            pltpu.VMEM((4, nz, cy, cx), F32),
-            pltpu.VMEM((4, parts, cy, cx), F32),
-            pltpu.VMEM((4, 2, parts, cy, cx), F32),
             pltpu.VMEM((nz, cy, cx), F32),
+            pltpu.VMEM((2, parts, cy, cx), F32),
+            pltpu.VMEM((2, 6, parts, cy, cx), F32),
             pltpu.VMEM((slots, points), BF16),
             pltpu.VMEM((nz * cy, slots), BF16),
             pltpu.VMEM((cx, slots), F32),
             pltpu.VMEM((3, groups // 2, 2, 128), F32),
             pltpu.VMEM((3, groups, 2, 128), F32),
-            pltpu.SemaphoreType.DMA((4, 4)),
-            pltpu.SemaphoreType.DMA((4, 4)),
+            pltpu.SemaphoreType.DMA((2, 16)),
+            pltpu.SemaphoreType.DMA((2, 16)),
             pltpu.SemaphoreType.DMA((3, groups)),
             pltpu.SemaphoreType.DMA((3, groups)),
             pltpu.SemaphoreType.DMA((9,)),

time: 49.2 us -> 46.4 us (0.943); the launches traced: 48.2 us -> 46.3 us
  Pallas kernels: 47.6 us -> 45.7 us
    pallas_call x1, Pallas kernels: 46.8 us -> 44.9 us  [per_device(): pl.pallas_call(functools.partial(kernel, groups, rows), out_shape=close,...]
where the time goes in v3:
time: 46.4 us; the launch traced here: 46.3 us
  Pallas kernels  45.7 us (98%)
  between operations  0.64 us (1%)
    pallas_call x1, Pallas kernels, per_device(): pl.pallas_call(functools.partial(kernel, groups, rows), out_shape=close,...  44.9 us

profile of v3, /device:TPU:1, one launch (start us, length us, event | category | flops | bytes accessed | tf_op | source)
XLA Modules:
  0.0 46.3 jit_solution(285057096906869228)
XLA Ops:
  0.6 44.9 %shard_map.120 = (f32[32,8,128]{2,1,0:T(8,128)S(1)}, f32[1,128]{1,0:T(1,128)S(1)}, f32[32,8,128]{2,1,0:T(8,128)S(1)}, f32[32,8,128]{2,1,0:T(8,128)S(1)}) custom-call(f32[32,8,128]{2,1,0:T(8,128)} %vt_hbm.1, f32[32,8,128]{2,1,0:T(8,128)} %wb_hbm.1, f32[32,8,128]{2,1,0:T(8,128)} %wn_hbm.1, f32[32,8,128]{2,1,0:T(8,128)} %al_hbm.1, f32[32,8,128]{2,1,0:T(8,128)} %an_hbm.1, ...), custom_call_target="tpu_custom_call" | custom-call | tf_op jit(solution)/shard_map/pallas_call | solution.py:593
  45.5 0.8 %shard_map.121 = (f32[32,8,128]{2,1,0:T(8,128)}, f32[1,128]{1,0:T(1,128)}, f32[32,8,128]{2,1,0:T(8,128)}, f32[32,8,128]{2,1,0:T(8,128)}) custom-call(f32[32,8,128]{2,1,0:T(8,128)S(1)} %get-tuple-element.12.refs_0_, f32[1,128]{1,0:T(1,128)S(1)} %get-tuple-element.13.refs_1_, f32[32,8,128]{2,1,0:T(8,128)S(1)} %get-tuple-element.14.refs_2_, ...), custom_call_target="tpu_custom_call" | custom-call | tf_op jit(solution)/shard_map/pallas_call | solution.py:650

commit v4 on v3

--- a/solution.py
+++ b/solution.py
@@ -77,8 +77,11 @@
     match,
     at_row,
     at_lane,
-    out_box,
-    in_box,
+    partner,
+    ask_out,
+    ask_in,
+    found_out,
+    found_in,
     face_send,
     face_recv,
     box_send,
@@ -325,27 +328,22 @@
     def box_copy(kind, d):
         to = lax.rem(gx + d, groups)
         return pltpu.make_async_remote_copy(
-            out_box.at[kind, to // 2],
-            in_box.at[kind, gx],
+            found_out if kind else ask_out.at[to // 2],
+            (found_in if kind else ask_in).at[gx],
             box_send.at[kind, d],
             box_recv.at[kind, d],
             device_id=(to, gy),
             device_id_type=MESH,
         )
 
-    def fill(kind, top, bottom):
-        for j in range(groups // 2):
-            piece = slice(128 * j, 128 * j + 128)
-            out_box[kind, j, 0:1] = top[:, piece]
-            out_box[kind, j, 1:2] = bottom[:, piece]
-
     def post(kind):
         for d in sorted(range(1, groups), key=far_first):
             box_copy(kind, d).start()
         boxes_out.append(kind)
-        in_box[kind, gx] = out_box[kind, gx // 2]
-
-    odd = lax.rem(gx, 2) == 1
+        if kind:
+            found_in[gx] = found_out[...]
+        else:
+            ask_in[gx] = ask_out[gx // 2]
 
     def collect(kind):
         def wait(d, carry):
@@ -353,16 +351,17 @@
             return carry
 
         lax.fori_loop(1, groups, wait, 0)
-        first, second = [], []
-        low = iota((2, 128), 1) < 64
+
+    def halves(box):
+        even, uneven = [], []
         for j in range(groups // 2):
-            a, b = in_box[kind, 2 * j], in_box[kind, 2 * j + 1]
-            a = jnp.where(odd, pltpu.roll(a, 64, 1), a)
-            b = jnp.where(odd, b, pltpu.roll(b, 64, 1))
-            both = jnp.where(low, a, b)
-            first.append(both[0:1])
-            second.append(both[1:2])
-        return jnp.concatenate(first, axis=1), jnp.concatenate(second, axis=1)
+            a, b = box[2 * j], box[2 * j + 1]
+            first = lax.broadcasted_iota(jnp.int32, a.shape, 1) < 64
+            even.append(jnp.where(first, a, pltpu.roll(b, 64, 1)))
+            uneven.append(jnp.where(first, pltpu.roll(a, 64, 1), b))
+        return jnp.concatenate(even, axis=1), jnp.concatenate(uneven, axis=1)
+
+    odd = lax.rem(gx, 2) == 1
 
     def rows_of(top, bottom):
         width = top.shape[1]
@@ -407,7 +406,7 @@
     pack(0, main_parts, SIDE, lambda z: vt_ref[z])
     pack(0, main_parts + side_parts, SIDE, lambda z: wb_ref[z])
     send(columns_side, 0)
-    for copy in loads[1:3]:
+    for copy in (*loads[1:3], *loads[5:7]):
         copy.wait()
 
     holder = hold_ref[...].astype(F32)
@@ -428,8 +427,26 @@
         match[s : s + 256] = jnp.where(
             (iota((256, points), 0) + s).astype(F32) == slot, 1.0, 0.0
         ).astype(BF16)
-    asked = nt(facts.astype(BF16), match[...])
-    fill(0, asked[1:2], asked[2:3])
+    other = [jnp.concatenate([x[:, half:], x[:, :half]], axis=1) for x in (holder, rank)]
+    coupling = coup_ref[...]
+    lines = [facts[1:2], facts[2:3], *other]
+    lines.append(jnp.where(iota((1, points), 1) < half, -1.0, 1.0))
+    for value in (coupling, obs_ref[0:1], obs_ref[1:2]):
+        for part in split3(value):
+            part = part.astype(F32)
+            lines.append(jnp.concatenate([part, part], axis=1))
+    at = iota((16, points), 0)
+    sheet = jnp.zeros((16, points), F32)
+    for i, line in enumerate(lines):
+        sheet = jnp.where(at == i, line, sheet)
+    asked = nt(sheet.astype(BF16), match[...])
+    lines = [asked[0:1], asked[1:2], asked[2:3] * cap + asked[3:4], asked[4:5]]
+    for i in (5, 8, 11):
+        lines.append((asked[i : i + 1] + asked[i + 1 : i + 2]) + asked[i + 2 : i + 3])
+    lines.append(asked[15:16])
+    for j in range(groups // 2):
+        for i, line in enumerate(lines):
+            ask_out[j, i : i + 1] = line[:, 128 * j : 128 * j + 128]
     post(0)
 
     take_main(0)
@@ -461,7 +478,10 @@
 
     lax.fori_loop(0, nz // STEP_Z, level_three, 0, unroll=True)
 
-    row, column = collect(0)
+    collect(0)
+    even, uneven = halves(ask_in)
+    told = jnp.where(odd, uneven, even)
+    row, column = told[0:1], told[1:2]
     for s in range(0, slots, 256):
         piece = slice(s, s + 256)
         at_row[:, piece] = jnp.where(
@@ -471,54 +491,59 @@
             iota((128, 256), 0).astype(F32) == column[:, piece], 1.0, 0.0
         )
 
-    def sample(values):
-        turned = values.reshape(nz * 8, 128).T
-        stacked = jnp.concatenate(split3(turned), axis=0)
-        found = []
-        for s in range(0, slots, 256):
-            piece = slice(s, s + 256)
-            got = nn(stacked, at_row[:, piece])
-            got = (got[0:128] + got[128:256]) + got[256:384]
-            found.append(jnp.sum(got * at_lane[:, piece], axis=0, keepdims=True))
-        return jnp.concatenate(found, axis=1)
-
-    sample_two = sample(field[1, pl.ds(PAD, nz)])
-
-    sample_last = sample(last[...])
-    fill(1, sample_two, sample_last)
+    next_last = jnp.concatenate(
+        [
+            part
+            for values in (field[1, inner], last[...])
+            for part in split3(values.reshape(nz * 8, 128).T)
+        ],
+        axis=0,
+    )
+    pieces = ([], [])
+    for s in range(0, slots, 256):
+        piece = slice(s, s + 256)
+        got = nn(next_last, at_row[:, piece])
+        for i, start in enumerate((0, 384)):
+            value = (got[start : start + 128] + got[start + 128 : start + 256]) + got[
+                start + 256 : start + 384
+            ]
+            pieces[i].append(jnp.sum(value * at_lane[:, piece], axis=0, keepdims=True))
+    mine = [jnp.concatenate(p, axis=1) for p in pieces]
+    for j in range(groups // 2):
+        for i in (0, 1):
+            found_out[2 * j + i : 2 * j + i + 1] = mine[i][:, 128 * j : 128 * j + 128]
     post(1)
 
-    two, three = collect(1)
-    for copy in loads[5:]:
+    key = told[2:3]
+    for s in range(0, slots, 256):
+        for c in range(0, slots, 256):
+            partner[s : s + 256, c : c + 256] = jnp.where(
+                (iota((256, 256), 0) + s).astype(F32) == key[:, c : c + 256], 1.0, 0.0
+            ).astype(BF16)
+    for copy in loads[7:]:
         copy.wait()
-    two, three = sum_rows(nn(rows_of(two, three), match[...]))
-    diff_two = two[:, half:] - two[:, :half]
-    diff_last = three[:, half:] - three[:, :half]
-    coupling = coup_ref[...]
-    error_two = coupling * diff_two - obs_ref[0:1]
-    error_last = coupling * diff_last - obs_ref[1:2]
-    gc_ref[...] = error_two * diff_two + error_last * diff_last
-    push_two = coupling * error_two
-    push_last = coupling * error_last
-    push = nt(
-        rows_of(
-            jnp.concatenate([-push_two, push_two], axis=1),
-            jnp.concatenate([-push_last, push_last], axis=1),
-        ),
-        match[...],
-    )
-    fill(2, *sum_rows(push))
-    post(2)
-
-    sources = collect(2)
+    collect(1)
+    even, uneven = halves(found_in)
+    got = nn(jnp.concatenate([*split3(even), *split3(uneven)], axis=0), partner[...])
+    n = groups
+    of_even = (got[0:n] + got[n : 2 * n]) + got[2 * n : 3 * n]
+    of_odd = (got[3 * n : 4 * n] + got[4 * n : 5 * n]) + got[5 * n : 6 * n]
+    line, place = iota((n, slots), 0), iota((n, slots), 1)
+    theirs = jnp.where(lax.rem(place, 128) < 64, of_even, of_odd)
+    sign, weight = told[3:4], told[4:5]
+    sources = []
+    for i in (0, 1):
+        kept = jnp.where(line == 2 * (place // 128) + i, theirs, 0.0)
+        diff = sign * (mine[i] - jnp.sum(kept, axis=0, keepdims=True))
+        error = weight * diff - told[5 + i : 6 + i]
+        sources.append(sign * (weight * error))
 
     def inject(source):
-        total = None
-        for part in split3(source):
-            spread = (at_lane[...] * part.astype(F32)).astype(BF16)
-            got = nt(at_row[...], spread)
-            total = got if total is None else total + got
-        return total.reshape(nz, 8, 128)
+        spread = jnp.concatenate(
+            [(at_lane[...] * part.astype(F32)).astype(BF16) for part in split3(source)], axis=0
+        )
+        got = nt(at_row[...], spread)
+        return ((got[:, 0:128] + got[:, 128:256]) + got[:, 256:384]).reshape(nz, 8, 128)
 
     three = al_ref[...] + inject(sources[1])
     adj3[...] = three
@@ -530,6 +555,18 @@
     send(rows_side, 1)
     pack(1, main_parts, SIDE, lambda z: known[z])
     send(columns_side, 1)
+    own = jnp.where(odd, uneven, even)
+    own = [
+        jnp.sum(jnp.where(line == 2 * (gx // 2) + i, own, 0.0), axis=0, keepdims=True)
+        for i in (0, 1)
+    ]
+    two, three = sum_rows(nn(rows_of(*own), match[...]))
+    diff_two = two[:, half:] - two[:, :half]
+    diff_last = three[:, half:] - three[:, :half]
+    error_two = coupling * diff_two - obs_ref[0:1]
+    error_last = coupling * diff_last - obs_ref[1:2]
+    gc_ref[...] = error_two * diff_two + error_last * diff_last
+
     take_main(1)
     take_sides(1)
 
@@ -620,12 +657,15 @@
             pltpu.VMEM((slots, points), BF16),
             pltpu.VMEM((nz * cy, slots), BF16),
             pltpu.VMEM((cx, slots), F32),
-            pltpu.VMEM((3, groups // 2, 2, 128), F32),
-            pltpu.VMEM((3, groups, 2, 128), F32),
+            pltpu.VMEM((slots, slots), BF16),
+            pltpu.VMEM((groups // 2, 8, 128), F32),
+            pltpu.VMEM((groups, 8, 128), F32),
+            pltpu.VMEM((groups, 128), F32),
+            pltpu.VMEM((groups, groups, 128), F32),
             pltpu.SemaphoreType.DMA((2, 16)),
             pltpu.SemaphoreType.DMA((2, 16)),
-            pltpu.SemaphoreType.DMA((3, groups)),
-            pltpu.SemaphoreType.DMA((3, groups)),
+            pltpu.SemaphoreType.DMA((2, groups)),
+            pltpu.SemaphoreType.DMA((2, groups)),
             pltpu.SemaphoreType.DMA((9,)),
         ],
         compiler_params=pltpu.CompilerParams(

time: 46.4 us -> 40.9 us (0.88)
  Pallas kernels: 45.7 us -> 40.2 us
    pallas_call x1, Pallas kernels: 44.9 us -> 39.4 us  [per_device(): pl.pallas_call(functools.partial(kernel, groups, rows), out_shape=close,...]
where the time goes in v4:
time: 40.9 us; the launch traced here: 40.8 us
  Pallas kernels  40.2 us (98%)
  between operations  0.64 us (2%)
    pallas_call x1, Pallas kernels, per_device(): pl.pallas_call(functools.partial(kernel, groups, rows), out_shape=close,...  39.4 us

profile of v4, /device:TPU:1, one launch (start us, length us, event | category | flops | bytes accessed | tf_op | source)
XLA Modules:
  0.0 40.8 jit_solution(15942666290598362542)
XLA Ops:
  0.6 39.4 %shard_map.120 = (f32[32,8,128]{2,1,0:T(8,128)S(1)}, f32[1,128]{1,0:T(1,128)S(1)}, f32[32,8,128]{2,1,0:T(8,128)S(1)}, f32[32,8,128]{2,1,0:T(8,128)S(1)}) custom-call(f32[32,8,128]{2,1,0:T(8,128)} %vt_hbm.1, f32[32,8,128]{2,1,0:T(8,128)} %wb_hbm.1, f32[32,8,128]{2,1,0:T(8,128)} %wn_hbm.1, f32[32,8,128]{2,1,0:T(8,128)} %al_hbm.1, f32[32,8,128]{2,1,0:T(8,128)} %an_hbm.1, ...), custom_call_target="tpu_custom_call" | custom-call | tf_op jit(solution)/shard_map/pallas_call | solution.py:630
  40.0 0.8 %shard_map.121 = (f32[32,8,128]{2,1,0:T(8,128)}, f32[1,128]{1,0:T(1,128)}, f32[32,8,128]{2,1,0:T(8,128)}, f32[32,8,128]{2,1,0:T(8,128)}) custom-call(f32[32,8,128]{2,1,0:T(8,128)S(1)} %get-tuple-element.12.refs_0_, f32[1,128]{1,0:T(1,128)S(1)} %get-tuple-element.13.refs_1_, f32[32,8,128]{2,1,0:T(8,128)S(1)} %get-tuple-element.14.refs_2_, ...), custom_call_target="tpu_custom_call" | custom-call | tf_op jit(solution)/shard_map/pallas_call | solution.py:690

commit v5 on v4

--- a/solution.py
+++ b/solution.py
@@ -35,6 +35,49 @@
 
 def nn(a, b):
     return lax.dot_general(a, b, (((1,), (0,)), ((), ())), preferred_element_type=F32)
+
+
+def levels(buffer, k, z, off):
+    return buffer[k, pl.ds(z + PAD + off, STEP_Z)]
+
+SHAPE = (STEP_Z, 8, 128)
+
+
+def cross(buffer, k, z, up, down, right, left):
+    total = (3.0 * STENCIL[0]) * levels(buffer, k, z, 0)
+    for off in range(1, 5):
+        near = levels(buffer, k, z, off) + levels(buffer, k, z, -off)
+        near += pltpu.roll(up(off), 8 - off, 1) + pltpu.roll(down(off), off, 1)
+        near += pltpu.roll(right(off), 128 - off, 2) + pltpu.roll(left(off), off, 2)
+        total += STENCIL[off] * near
+    return total
+
+
+def across_x(inside, outside):
+    lane3 = iota(SHAPE, 2)
+    return (
+        lambda off: jnp.where(lane3 < off, outside, inside),
+        lambda off: jnp.where(lane3 >= 128 - off, outside, inside),
+    )
+
+
+def across_y(inside, outside):
+    sub3 = iota(SHAPE, 1)
+    return (
+        lambda off: jnp.where(sub3 < off, outside, inside),
+        lambda off: jnp.where(sub3 >= 8 - off, outside, inside),
+    )
+
+
+def on_block(field, strip_y, strip_x, k, z):
+    own = levels(field, k, z, 0)
+    return cross(
+        field,
+        k,
+        z,
+        *across_y(own, levels(strip_y, k, z, 0)),
+        *across_x(own, levels(strip_x, k, z, 0)),
+    )
 
 
 def kernel(
@@ -51,8 +94,9 @@
     obs_hbm,
     gv_ref,
     gc_ref,
-    ae_ref,
     am_ref,
+    adj3,
+    ends,
     vt_ref,
     wb_ref,
     al_ref,
@@ -71,7 +115,6 @@
     lap,
     last,
     known,
-    adj3,
     x_send,
     x_recv,
     match,
@@ -163,8 +206,8 @@
         )
 
     low, high, inner = pl.ds(0, 4), pl.ds(4, 4), pl.ds(PAD, nz)
-    mains = (wn_hbm, field.at[2, inner])
-    sides = (((vt_hbm, 0), (wb_hbm, 1)), ((known, 2),))
+    mains = (field.at[0, inner], field.at[2, inner])
+    sides = (((vt_ref, 0), (wb_ref, 1)), ((known, 2),))
     below, above = (gx, y_prev), (gx, y_next)
 
     def rows_main(e):
@@ -258,43 +301,6 @@
                 to_side,
             )
 
-    def levels(buffer, k, z, off):
-        return buffer[k, pl.ds(z + PAD + off, STEP_Z)]
-
-    shape3 = (STEP_Z, 8, 128)
-    lane3, sub3 = iota(shape3, 2), iota(shape3, 1)
-
-    def cross(buffer, k, z, up, down, right, left):
-        total = (3.0 * STENCIL[0]) * levels(buffer, k, z, 0)
-        for off in range(1, 5):
-            near = levels(buffer, k, z, off) + levels(buffer, k, z, -off)
-            near += pltpu.roll(up(off), 8 - off, 1) + pltpu.roll(down(off), off, 1)
-            near += pltpu.roll(right(off), 128 - off, 2) + pltpu.roll(left(off), off, 2)
-            total += STENCIL[off] * near
-        return total
-
-    def across_x(inside, outside):
-        return (
-            lambda off: jnp.where(lane3 < off, outside, inside),
-            lambda off: jnp.where(lane3 >= 128 - off, outside, inside),
-        )
-
-    def across_y(inside, outside):
-        return (
-            lambda off: jnp.where(sub3 < off, outside, inside),
-            lambda off: jnp.where(sub3 >= 8 - off, outside, inside),
-        )
-
-    def on_block(k, z):
-        own = levels(field, k, z, 0)
-        return cross(
-            field,
-            k,
-            z,
-            *across_y(own, levels(strip_y, k, z, 0)),
-            *across_x(own, levels(strip_x, k, z, 0)),
-        )
-
     def on_strip_x(k, z):
         own, strip = levels(field, k, z, 0), levels(strip_x, k, z, 0)
         return cross(
@@ -306,6 +312,7 @@
         )
 
     def on_strip_y(k, z):
+        sub3 = iota(SHAPE, 1)
         own, strip = levels(field, k, z, 0), levels(strip_y, k, z, 0)
         far = far_y[k // 2, pl.ds(z, STEP_Z)]
 
@@ -392,17 +399,17 @@
         lax.fori_loop(1, groups, gone, 0)
 
     pl.semaphore_wait(barrier, groups + 5)
-    send(rows_main, 0)
-    send(rows_side, 0)
-    for buffer, used in ((field, range(4)), (strip_y, (0, 2)), (strip_x, (0, 2))):
+    for buffer, used in ((field, range(3)), (ends, (0,)), (strip_y, (0, 2)), (strip_x, (0, 2))):
         for k in used:
             buffer[k, 0:PAD] = jnp.zeros((PAD, 8, 128), F32)
             buffer[k, pl.ds(nz + PAD, PAD)] = jnp.zeros((PAD, 8, 128), F32)
     loads[0].wait()
+    send(rows_main, 0)
     pack(0, 0, MAIN, lambda z: field[0, PAD + z])
     send(columns_main, 0)
     for copy in loads[3:5]:
         copy.wait()
+    send(rows_side, 0)
     pack(0, main_parts, SIDE, lambda z: vt_ref[z])
     pack(0, main_parts + side_parts, SIDE, lambda z: wb_ref[z])
     send(columns_side, 0)
@@ -450,34 +457,19 @@
     post(0)
 
     take_main(0)
-    take_sides(0)
 
     def level_two(c, carry):
         z = c * STEP_Z
         here = pl.ds(z, STEP_Z)
         put = pl.ds(z + PAD, STEP_Z)
-        one = on_block(0, z)
+        one = on_block(field, strip_y, strip_x, 0, z)
         lap[0, here] = one
         field[1, put] = 2.0 * field[0, put] - wb_ref[here] + vt_ref[here] * one
-        value = 2.0 * strip_y[0, put] - side_y[1, here] + side_y[0, here] * on_strip_y(0, z)
-        strip_y[1, put] = jnp.where(y_inside[None], value, 0.0)
-        value = 2.0 * strip_x[0, put] - side_x[1, here] + side_x[0, here] * on_strip_x(0, z)
-        strip_x[1, put] = jnp.where(x_inside[None], value, 0.0)
+        strip_y[1, put] = on_strip_y(0, z)
+        strip_x[1, put] = on_strip_x(0, z)
         return carry
 
     lax.fori_loop(0, nz // STEP_Z, level_two, 0, unroll=True)
-
-    def level_three(c, carry):
-        z = c * STEP_Z
-        here = pl.ds(z, STEP_Z)
-        put = pl.ds(z + PAD, STEP_Z)
-        two = on_block(1, z)
-        lap[1, here] = two
-        last[here] = 2.0 * field[1, put] - field[0, put] + vt_ref[here] * two
-        return carry
-
-    lax.fori_loop(0, nz // STEP_Z, level_three, 0, unroll=True)
-
     collect(0)
     even, uneven = halves(ask_in)
     told = jnp.where(odd, uneven, even)
@@ -491,24 +483,41 @@
             iota((128, 256), 0).astype(F32) == column[:, piece], 1.0, 0.0
         )
 
-    next_last = jnp.concatenate(
-        [
-            part
-            for values in (field[1, inner], last[...])
-            for part in split3(values.reshape(nz * 8, 128).T)
-        ],
-        axis=0,
-    )
-    pieces = ([], [])
-    for s in range(0, slots, 256):
-        piece = slice(s, s + 256)
-        got = nn(next_last, at_row[:, piece])
-        for i, start in enumerate((0, 384)):
-            value = (got[start : start + 128] + got[start + 128 : start + 256]) + got[
-                start + 256 : start + 384
-            ]
-            pieces[i].append(jnp.sum(value * at_lane[:, piece], axis=0, keepdims=True))
-    mine = [jnp.concatenate(p, axis=1) for p in pieces]
+    def sample(values):
+        parts3 = jnp.concatenate(split3(values.reshape(nz * 8, 128).T), axis=0)
+        pieces = []
+        for s in range(0, slots, 256):
+            piece = slice(s, s + 256)
+            got = nn(parts3, at_row[:, piece])
+            got = (got[0:128] + got[128:256]) + got[256:384]
+            pieces.append(jnp.sum(got * at_lane[:, piece], axis=0, keepdims=True))
+        return jnp.concatenate(pieces, axis=1)
+
+    mine = [sample(field[1, inner])]
+    take_sides(0)
+
+    def strips_two(c, carry):
+        here = pl.ds(c * STEP_Z, STEP_Z)
+        put = pl.ds(c * STEP_Z + PAD, STEP_Z)
+        for strip, side, inside in ((strip_y, side_y, y_inside), (strip_x, side_x, x_inside)):
+            value = 2.0 * strip[0, put] - side[1, here] + side[0, here] * strip[1, put]
+            strip[1, put] = jnp.where(inside[None], value, 0.0)
+        return carry
+
+    lax.fori_loop(0, nz // STEP_Z, strips_two, 0, unroll=True)
+
+    def level_three(c, carry):
+        z = c * STEP_Z
+        here = pl.ds(z, STEP_Z)
+        put = pl.ds(z + PAD, STEP_Z)
+        two = on_block(field, strip_y, strip_x, 1, z)
+        lap[1, here] = two
+        last[here] = 2.0 * field[1, put] - field[0, put] + vt_ref[here] * two
+        return carry
+
+    lax.fori_loop(0, nz // STEP_Z, level_three, 0, unroll=True)
+
+    mine.append(sample(last[...]))
     for j in range(groups // 2):
         for i in (0, 1):
             found_out[2 * j + i : 2 * j + i + 1] = mine[i][:, 128 * j : 128 * j + 128]
@@ -531,27 +540,27 @@
     line, place = iota((n, slots), 0), iota((n, slots), 1)
     theirs = jnp.where(lax.rem(place, 128) < 64, of_even, of_odd)
     sign, weight = told[3:4], told[4:5]
-    sources = []
-    for i in (0, 1):
+
+    def source(i):
         kept = jnp.where(line == 2 * (place // 128) + i, theirs, 0.0)
         diff = sign * (mine[i] - jnp.sum(kept, axis=0, keepdims=True))
         error = weight * diff - told[5 + i : 6 + i]
-        sources.append(sign * (weight * error))
-
-    def inject(source):
+        return sign * (weight * error)
+
+    def inject(strength):
         spread = jnp.concatenate(
-            [(at_lane[...] * part.astype(F32)).astype(BF16) for part in split3(source)], axis=0
+            [(at_lane[...] * part.astype(F32)).astype(BF16) for part in split3(strength)], axis=0
         )
         got = nt(at_row[...], spread)
         return ((got[:, 0:128] + got[:, 128:256]) + got[:, 256:384]).reshape(nz, 8, 128)
 
-    three = al_ref[...] + inject(sources[1])
+    three = al_ref[...] + inject(source(1))
     adj3[...] = three
     field[2, inner] = vt_ref[...] * three
     send(rows_main, 1)
     pack(1, 0, MAIN, lambda z: field[2, PAD + z])
     send(columns_main, 1)
-    known[...] = an_ref[...] + inject(sources[0]) + 2.0 * adj3[...]
+    known[...] = an_ref[...] + inject(source(0)) + 2.0 * adj3[...]
     send(rows_side, 1)
     pack(1, main_parts, SIDE, lambda z: known[z])
     send(columns_side, 1)
@@ -568,39 +577,57 @@
     gc_ref[...] = error_two * diff_two + error_last * diff_last
 
     take_main(1)
-    take_sides(1)
 
     def adjoint_two(c, carry):
         z = c * STEP_Z
         here = pl.ds(z, STEP_Z)
         put = pl.ds(z + PAD, STEP_Z)
-        middle = known[here] + on_block(2, z)
+        middle = known[here] + on_block(field, strip_y, strip_x, 2, z)
         am_ref[here] = middle
-        field[3, put] = vt_ref[here] * middle
-        value = side_y[0, here] * (side_y[2, here] + on_strip_y(2, z))
-        strip_y[3, put] = jnp.where(y_inside[None], value, 0.0)
-        value = side_x[0, here] * (side_x[2, here] + on_strip_x(2, z))
-        strip_x[3, put] = jnp.where(x_inside[None], value, 0.0)
+        ends[0, put] = vt_ref[here] * middle
+        ends[1, put] = on_strip_y(2, z)
+        ends[2, put] = on_strip_x(2, z)
         gv_ref[here] = adj3[here] * lap[1, here] + middle * lap[0, here]
         return carry
 
     lax.fori_loop(0, nz // STEP_Z, adjoint_two, 0, unroll=True)
-
-    def adjoint_one(c, carry):
-        z = c * STEP_Z
-        here = pl.ds(z, STEP_Z)
-        ae_ref[here] = 2.0 * am_ref[here] - adj3[here] + on_block(3, z)
+    take_sides(1)
+
+    def strips_one(c, carry):
+        here = pl.ds(c * STEP_Z, STEP_Z)
+        put = pl.ds(c * STEP_Z + PAD, STEP_Z)
+        for i, side, inside in ((1, side_y, y_inside), (2, side_x, x_inside)):
+            value = side[0, here] * (side[2, here] + ends[i, put])
+            ends[i, put] = jnp.where(inside[None], value, 0.0)
         return carry
 
-    lax.fori_loop(0, nz // STEP_Z, adjoint_one, 0, unroll=True)
+    lax.fori_loop(0, nz // STEP_Z, strips_one, 0, unroll=True)
+
     finish()
 
 
-def write_kernel(*refs):
-    near, far, sem = refs[:4], refs[4:8], refs[8]
-    copies = [pltpu.make_async_copy(near[i], far[i], sem.at[i]) for i in range(4)]
+def write_kernel(gv_ref, gc_ref, am_ref, adj3, ends, gv_out, gc_out, ae_out, am_out, ae_ref, sem):
+    copies = [
+        pltpu.make_async_copy(near, far, sem.at[i])
+        for i, (near, far) in enumerate(((gv_ref, gv_out), (am_ref, am_out), (gc_ref, gc_out)))
+    ]
     for copy in copies:
         copy.start()
+    nz = ae_ref.shape[0]
+    own, strip_y, strip_x = (ends.at[pl.ds(i, 1)] for i in range(3))
+    for part in range(2):
+
+        def adjoint_one(c, carry):
+            z = c * STEP_Z
+            here = pl.ds(z, STEP_Z)
+            ae_ref[here] = 2.0 * am_ref[here] - adj3[here] + on_block(own, strip_y, strip_x, 0, z)
+            return carry
+
+        steps = nz // (2 * STEP_Z)
+        lax.fori_loop(part * steps, part * steps + steps, adjoint_one, 0, unroll=True)
+        done = pl.ds(part * (nz // 2), nz // 2)
+        copies.append(pltpu.make_async_copy(ae_ref.at[done], ae_out.at[done], sem.at[3 + part]))
+        copies[-1].start()
     for copy in copies:
         copy.wait()
 
@@ -626,12 +653,13 @@
     vmem = pl.BlockSpec(memory_space=pltpu.VMEM)
     hbm = pl.BlockSpec(memory_space=pltpu.HBM)
     found = (block, jax.ShapeDtypeStruct((1, channels), F32), block, block)
-    close = tuple(pltpu.VMEM(leaf.shape, leaf.dtype) for leaf in found)
+    close = [pltpu.VMEM((nz, cy, cx), F32), pltpu.VMEM((1, channels), F32)]
+    close += [pltpu.VMEM((nz, cy, cx), F32)] * 2 + [pltpu.VMEM((3, nz + 2 * PAD, cy, cx), F32)]
     near = pl.pallas_call(
         functools.partial(kernel, groups, rows),
-        out_shape=close,
+        out_shape=tuple(close),
         in_specs=[hbm] * 9,
-        out_specs=[vmem] * 4,
+        out_specs=[vmem] * 5,
         scratch_shapes=[
             pltpu.VMEM((nz, cy, cx), F32),
             pltpu.VMEM((nz, cy, cx), F32),
@@ -649,7 +677,6 @@
             pltpu.VMEM((3, nz, cy, cx), F32),
             pltpu.VMEM((3, nz, cy, cx), F32),
             pltpu.VMEM((2, nz, cy, cx), F32),
-            pltpu.VMEM((nz, cy, cx), F32),
             pltpu.VMEM((nz, cy, cx), F32),
             pltpu.VMEM((nz, cy, cx), F32),
             pltpu.VMEM((2, parts, cy, cx), F32),
@@ -690,9 +717,9 @@
     grad_velocity, grad_coupling, adjoint_early, adjoint_middle = pl.pallas_call(
         write_kernel,
         out_shape=found,
-        in_specs=[vmem] * 4,
+        in_specs=[vmem] * 5,
         out_specs=[hbm] * 4,
-        scratch_shapes=[pltpu.SemaphoreType.DMA((4,))],
+        scratch_shapes=[pltpu.VMEM((nz, cy, cx), F32), pltpu.SemaphoreType.DMA((5,))],
     )(*(pltpu.with_memory_space_constraint(x, pltpu.VMEM) for x in near))
     return grad_velocity, grad_coupling.reshape(channels), adjoint_early, adjoint_middle
 

time: 40.9 us -> 40 us (0.978)
  Pallas kernels: 40.2 us -> 39.2 us
    pallas_call x2, Pallas kernels: 40.2 us -> 39.2 us  [the longest x1 38.2 us: per_device(): pl.pallas_call(functools.partial(kernel, groups, rows), out_shape=tuple(c...]
where the time goes in v5:
time: 40 us; the launch traced here: 39.9 us
  Pallas kernels  39.2 us (98%)
  between operations  0.64 us (2%)
    pallas_call x1, Pallas kernels, per_device(): pl.pallas_call(functools.partial(kernel, groups, rows), out_shape=tuple(c...  38.2 us
    pallas_call x1, Pallas kernels, per_device(): pl.pallas_call(write_kernel, out_shape=found, in_specs=[vmem] * 5, out_sp...  1.03 us

profile of v5, /device:TPU:1, one launch (start us, length us, event | category | flops | bytes accessed | tf_op | source)
XLA Modules:
  0.0 39.9 jit_solution(2060620689562338880)
XLA Ops:
  0.6 38.2 %shard_map.120 = (f32[32,8,128]{2,1,0:T(8,128)S(1)}, f32[1,128]{1,0:T(1,128)S(1)}, f32[32,8,128]{2,1,0:T(8,128)S(1)}, f32[32,8,128]{2,1,0:T(8,128)S(1)}, f32[3,40,8,128]{3,2,1,0:T(8,128)S(1)}) custom-call(f32[32,8,128]{2,1,0:T(8,128)} %vt_hbm.1, f32[32,8,128]{2,1,0:T(8,128)} %wb_hbm.1, f32[32,8,128]{2,1,0:T(8,128)} %wn_hbm.1, f32[32,8,128]{2,1,0:T(8,128)} %al_hbm.1, ...), custom_call_target="tpu_custom_call" | custom-call | tf_op jit(solution)/shard_map/pallas_call | solution.py:658
  38.8 1.0 %shard_map.121 = (f32[32,8,128]{2,1,0:T(8,128)}, f32[1,128]{1,0:T(1,128)}, f32[32,8,128]{2,1,0:T(8,128)}, f32[32,8,128]{2,1,0:T(8,128)}) custom-call(f32[32,8,128]{2,1,0:T(8,128)S(1)} %get-tuple-element.13.gv_ref, f32[1,128]{1,0:T(1,128)S(1)} %get-tuple-element.14.gc_ref, f32[32,8,128]{2,1,0:T(8,128)S(1)} %get-tuple-element.15.am_ref, ...), custom_call_target="tpu_custom_call" | custom-call | tf_op jit(solution)/shard_map/pallas_call | solution.py:717

commit v6 on v5

--- a/solution.py
+++ b/solution.py
@@ -141,6 +141,20 @@
     x_prev, x_next = lax.rem(gx + groups - 1, groups), lax.rem(gx + 1, groups)
     y_prev, y_next = lax.rem(gy + rows - 1, rows), lax.rem(gy + 1, rows)
 
+    barrier = pltpu.get_barrier_semaphore()
+
+    def far_first(d):
+        step = d % 8
+        return -min(step, 8 - step), d
+
+    for d in sorted(range(1, groups), key=far_first):
+        pl.semaphore_signal(
+            barrier, inc=1, device_id=(lax.rem(gx + d, groups), gy), device_id_type=MESH
+        )
+    for x in (x_prev, x_next, gx):
+        for y in (y_prev, y_next):
+            pl.semaphore_signal(barrier, inc=1, device_id=(x, y), device_id_type=MESH)
+
     wn_ref = field.at[0, pl.ds(PAD, nz)]
     loads = [
         pltpu.make_async_copy(far, near, load_sem.at[i])
@@ -161,22 +175,6 @@
     for copy in loads:
         copy.start()
 
-    barrier = pltpu.get_barrier_semaphore()
-
-    def greet(d, carry):
-        pl.semaphore_signal(
-            barrier, inc=1, device_id=(lax.rem(gx + d, groups), gy), device_id_type=MESH
-        )
-        return carry
-
-    lax.fori_loop(1, groups, greet, 0)
-    for other in (y_prev, y_next):
-        pl.semaphore_signal(barrier, inc=1, device_id=(gx, other), device_id_type=MESH)
-
-    for x in (x_prev, x_next):
-        for y in (y_prev, y_next):
-            pl.semaphore_signal(barrier, inc=1, device_id=(x, y), device_id_type=MESH)
-
     lane = iota((8, 128), 1)
     sub = iota((8, 128), 0)
 
@@ -210,11 +208,16 @@
     sides = (((vt_ref, 0), (wb_ref, 1)), ((known, 2),))
     below, above = (gx, y_prev), (gx, y_next)
 
-    def rows_main(e):
-        near, far = strip_y.at[2 * e, inner], far_y.at[e]
+    def rows_near(e):
+        near = strip_y.at[2 * e, inner]
         return [
             remote(mains[e].at[:, low], near.at[:, low], e, 0, below),
             remote(mains[e].at[:, high], near.at[:, high], e, 1, above),
+        ]
+
+    def rows_far(e):
+        far = far_y.at[e]
+        return [
             remote(mains[e].at[:, high], far.at[:, high], e, 2, below),
             remote(mains[e].at[:, low], far.at[:, low], e, 3, above),
         ]
@@ -229,10 +232,21 @@
             ]
         return copies
 
-    def columns_main(e):
+    def columns_main(e, diagonal):
         part = pl.ds(0, main_parts)
         to = ((x_next, gy), (x_prev, gy), (x_next, y_next), (x_next, y_prev), (x_prev, y_next), (x_prev, y_prev))
-        return [remote(x_send.at[e, part], x_recv.at[e, i, part], e, 8 + i, to[i]) for i in (2, 3, 4, 5, 0, 1)]
+        copies = []
+        for i in (2, 3, 4, 5) if diagonal else (0, 1):
+            half = (high, low)[i % 2] if diagonal else pl.ds(0, 8)
+            source, target = x_send.at[e, part, half], x_recv.at[e, i, part, half]
+            copies.append(remote(source, target, e, 8 + i, to[i]))
+        return copies
+
+    def columns_diagonal(e):
+        return columns_main(e, True)
+
+    def columns_straight(e):
+        return columns_main(e, False)
 
     def columns_side(e):
         part = pl.ds(main_parts, side_parts * len(sides[e]))
@@ -251,38 +265,54 @@
     y_inside = ((sub < 4) & (gy < rows - 1)) | ((sub >= 4) & (gy > 0))
     x_inside = ((lane >= 64) & (gx > 0)) | ((lane < 64) & (gx < groups - 1))
 
-    def take_main(e):
-        take(rows_main, e)
+    left = lax.rem(lane, MAIN) < MAIN // 2
+    exists = (left & (gx > 0)) | (jnp.logical_not(left) & (gx < groups - 1))
+
+    def take_near(e):
+        take(rows_near, e)
+        take(columns_straight, e)
 
         @pl.when(gy == 0)
         def _():
             strip_y[2 * e, inner, high] = jnp.zeros((nz, 4, 128), F32)
-            far_y[e, :, low] = jnp.zeros((nz, 4, 128), F32)
 
         @pl.when(gy == rows - 1)
         def _():
             strip_y[2 * e, inner, low] = jnp.zeros((nz, 4, 128), F32)
+
+        straight = [
+            jnp.where(exists, jnp.where(left, x_recv[e, 0, part], x_recv[e, 1, part]), 0.0)
+            for part in range(main_parts)
+        ]
+
+        def to_strip(z, value):
+            strip_x[2 * e, PAD + z] = value
+
+        unpack(MAIN, straight, to_strip)
+
+    def take_far(e):
+        take(rows_far, e)
+        take(columns_diagonal, e)
+
+        @pl.when(gy == 0)
+        def _():
+            far_y[e, :, low] = jnp.zeros((nz, 4, 128), F32)
+
+        @pl.when(gy == rows - 1)
+        def _():
             far_y[e, :, high] = jnp.zeros((nz, 4, 128), F32)
 
-        take(columns_main, e)
-        left = lax.rem(lane, MAIN) < MAIN // 2
-        exists = (left & (gx > 0)) | (jnp.logical_not(left) & (gx < groups - 1))
-        straight, across = [], []
+        across = []
         for part in range(main_parts):
-            got = [x_recv[e, i, part] for i in range(6)]
-            straight.append(jnp.where(exists, jnp.where(left, got[0], got[1]), 0.0))
+            got = [x_recv[e, i, part] for i in range(2, 6)]
             diagonal = jnp.where(
-                left, jnp.where(sub < 4, got[3], got[2]), jnp.where(sub < 4, got[5], got[4])
+                left, jnp.where(sub < 4, got[1], got[0]), jnp.where(sub < 4, got[3], got[2])
             )
             across.append(jnp.where(exists & y_inside, diagonal, 0.0))
 
-        def to_strip(z, value):
-            strip_x[2 * e, PAD + z] = value
-
         def to_corner(z, value):
             corner[e, z] = value
 
-        unpack(MAIN, straight, to_strip)
         unpack(MAIN, across, to_corner)
 
     def take_sides(e):
@@ -328,15 +358,11 @@
             strip_y, k, z, up, down, *across_x(strip, corner[k // 2, pl.ds(z, STEP_Z)])
         )
 
-    def far_first(d):
-        step = d % 8
-        return -min(step, 8 - step), d
-
     def box_copy(kind, d):
         to = lax.rem(gx + d, groups)
         return pltpu.make_async_remote_copy(
-            found_out if kind else ask_out.at[to // 2],
-            (found_in if kind else ask_in).at[gx],
+            found_out.at[kind - 1] if kind else ask_out.at[to // 2],
+            found_in.at[kind - 1, gx] if kind else ask_in.at[gx],
             box_send.at[kind, d],
             box_recv.at[kind, d],
             device_id=(to, gy),
@@ -348,7 +374,7 @@
             box_copy(kind, d).start()
         boxes_out.append(kind)
         if kind:
-            found_in[gx] = found_out[...]
+            found_in[kind - 1, gx] = found_out[kind - 1]
         else:
             ask_in[gx] = ask_out[gx // 2]
 
@@ -404,9 +430,11 @@
             buffer[k, 0:PAD] = jnp.zeros((PAD, 8, 128), F32)
             buffer[k, pl.ds(nz + PAD, PAD)] = jnp.zeros((PAD, 8, 128), F32)
     loads[0].wait()
-    send(rows_main, 0)
+    send(rows_near, 0)
+    send(rows_far, 0)
     pack(0, 0, MAIN, lambda z: field[0, PAD + z])
-    send(columns_main, 0)
+    send(columns_diagonal, 0)
+    send(columns_straight, 0)
     for copy in loads[3:5]:
         copy.wait()
     send(rows_side, 0)
@@ -456,7 +484,7 @@
             ask_out[j, i : i + 1] = line[:, 128 * j : 128 * j + 128]
     post(0)
 
-    take_main(0)
+    take_near(0)
 
     def level_two(c, carry):
         z = c * STEP_Z
@@ -465,11 +493,19 @@
         one = on_block(field, strip_y, strip_x, 0, z)
         lap[0, here] = one
         field[1, put] = 2.0 * field[0, put] - wb_ref[here] + vt_ref[here] * one
+        return carry
+
+    lax.fori_loop(0, nz // STEP_Z, level_two, 0, unroll=True)
+    take_far(0)
+
+    def around_two(c, carry):
+        z = c * STEP_Z
+        put = pl.ds(z + PAD, STEP_Z)
         strip_y[1, put] = on_strip_y(0, z)
         strip_x[1, put] = on_strip_x(0, z)
         return carry
 
-    lax.fori_loop(0, nz // STEP_Z, level_two, 0, unroll=True)
+    lax.fori_loop(0, nz // STEP_Z, around_two, 0, unroll=True)
     collect(0)
     even, uneven = halves(ask_in)
     told = jnp.where(odd, uneven, even)
@@ -493,7 +529,13 @@
             pieces.append(jnp.sum(got * at_lane[:, piece], axis=0, keepdims=True))
         return jnp.concatenate(pieces, axis=1)
 
-    mine = [sample(field[1, inner])]
+    def tell(i, found):
+        for j in range(groups // 2):
+            found_out[i, j : j + 1] = found[:, 128 * j : 128 * j + 128]
+        post(1 + i)
+        return found
+
+    mine = [tell(0, sample(field[1, inner]))]
     take_sides(0)
 
     def strips_two(c, carry):
@@ -517,12 +559,7 @@
 
     lax.fori_loop(0, nz // STEP_Z, level_three, 0, unroll=True)
 
-    mine.append(sample(last[...]))
-    for j in range(groups // 2):
-        for i in (0, 1):
-            found_out[2 * j + i : 2 * j + i + 1] = mine[i][:, 128 * j : 128 * j + 128]
-    post(1)
-
+    mine.append(tell(1, sample(last[...])))
     key = told[2:3]
     for s in range(0, slots, 256):
         for c in range(0, slots, 256):
@@ -531,21 +568,21 @@
             ).astype(BF16)
     for copy in loads[7:]:
         copy.wait()
-    collect(1)
-    even, uneven = halves(found_in)
-    got = nn(jnp.concatenate([*split3(even), *split3(uneven)], axis=0), partner[...])
-    n = groups
-    of_even = (got[0:n] + got[n : 2 * n]) + got[2 * n : 3 * n]
-    of_odd = (got[3 * n : 4 * n] + got[4 * n : 5 * n]) + got[5 * n : 6 * n]
-    line, place = iota((n, slots), 0), iota((n, slots), 1)
-    theirs = jnp.where(lax.rem(place, 128) < 64, of_even, of_odd)
+    line, place = iota((groups, slots), 0), iota((groups, slots), 1)
+    theirs_at = place // 128 + groups // 2 * (lax.rem(place, 128) // 64)
     sign, weight = told[3:4], told[4:5]
 
     def source(i):
-        kept = jnp.where(line == 2 * (place // 128) + i, theirs, 0.0)
-        diff = sign * (mine[i] - jnp.sum(kept, axis=0, keepdims=True))
+        collect(1 + i)
+        even, uneven = halves(found_in.at[i])
+        got = nn(jnp.concatenate(split3(jnp.concatenate([even, uneven], axis=0)), axis=0), partner[...])
+        got = (got[0:groups] + got[groups : 2 * groups]) + got[2 * groups :]
+        theirs = jnp.sum(jnp.where(line == theirs_at, got, 0.0), axis=0, keepdims=True)
+        diff = sign * (mine[i] - theirs)
         error = weight * diff - told[5 + i : 6 + i]
-        return sign * (weight * error)
+        own = jnp.where(odd, uneven, even)
+        own = jnp.where(iota(own.shape, 0) == gx // 2, own, 0.0)
+        return sign * (weight * error), jnp.sum(own, axis=0, keepdims=True)
 
     def inject(strength):
         spread = jnp.concatenate(
@@ -554,29 +591,29 @@
         got = nt(at_row[...], spread)
         return ((got[:, 0:128] + got[:, 128:256]) + got[:, 256:384]).reshape(nz, 8, 128)
 
-    three = al_ref[...] + inject(source(1))
+    strength, own_two = source(0)
+    known[...] = an_ref[...] + inject(strength)
+    strength, own_last = source(1)
+    three = al_ref[...] + inject(strength)
     adj3[...] = three
     field[2, inner] = vt_ref[...] * three
-    send(rows_main, 1)
+    send(rows_near, 1)
+    send(rows_far, 1)
     pack(1, 0, MAIN, lambda z: field[2, PAD + z])
-    send(columns_main, 1)
-    known[...] = an_ref[...] + inject(source(0)) + 2.0 * adj3[...]
+    send(columns_diagonal, 1)
+    send(columns_straight, 1)
+    known[...] += 2.0 * adj3[...]
     send(rows_side, 1)
     pack(1, main_parts, SIDE, lambda z: known[z])
     send(columns_side, 1)
-    own = jnp.where(odd, uneven, even)
-    own = [
-        jnp.sum(jnp.where(line == 2 * (gx // 2) + i, own, 0.0), axis=0, keepdims=True)
-        for i in (0, 1)
-    ]
-    two, three = sum_rows(nn(rows_of(*own), match[...]))
+    two, three = sum_rows(nn(rows_of(own_two, own_last), match[...]))
     diff_two = two[:, half:] - two[:, :half]
     diff_last = three[:, half:] - three[:, :half]
     error_two = coupling * diff_two - obs_ref[0:1]
     error_last = coupling * diff_last - obs_ref[1:2]
     gc_ref[...] = error_two * diff_two + error_last * diff_last
 
-    take_main(1)
+    take_near(1)
 
     def adjoint_two(c, carry):
         z = c * STEP_Z
@@ -585,12 +622,20 @@
         middle = known[here] + on_block(field, strip_y, strip_x, 2, z)
         am_ref[here] = middle
         ends[0, put] = vt_ref[here] * middle
+        gv_ref[here] = adj3[here] * lap[1, here] + middle * lap[0, here]
+        return carry
+
+    lax.fori_loop(0, nz // STEP_Z, adjoint_two, 0, unroll=True)
+    take_far(1)
+
+    def around_one(c, carry):
+        z = c * STEP_Z
+        put = pl.ds(z + PAD, STEP_Z)
         ends[1, put] = on_strip_y(2, z)
         ends[2, put] = on_strip_x(2, z)
-        gv_ref[here] = adj3[here] * lap[1, here] + middle * lap[0, here]
         return carry
 
-    lax.fori_loop(0, nz // STEP_Z, adjoint_two, 0, unroll=True)
+    lax.fori_loop(0, nz // STEP_Z, around_one, 0, unroll=True)
     take_sides(1)
 
     def strips_one(c, carry):
@@ -687,12 +732,12 @@
             pltpu.VMEM((slots, slots), BF16),
             pltpu.VMEM((groups // 2, 8, 128), F32),
             pltpu.VMEM((groups, 8, 128), F32),
-            pltpu.VMEM((groups, 128), F32),
-            pltpu.VMEM((groups, groups, 128), F32),
+            pltpu.VMEM((2, groups // 2, 128), F32),
+            pltpu.VMEM((2, groups, groups // 2, 128), F32),
             pltpu.SemaphoreType.DMA((2, 16)),
             pltpu.SemaphoreType.DMA((2, 16)),
-            pltpu.SemaphoreType.DMA((2, groups)),
-            pltpu.SemaphoreType.DMA((2, groups)),
+            pltpu.SemaphoreType.DMA((3, groups)),
+            pltpu.SemaphoreType.DMA((3, groups)),
             pltpu.SemaphoreType.DMA((9,)),
         ],
         compiler_params=pltpu.CompilerParams(

time: 40 us -> 39.3 us (0.982)
  Pallas kernels: 39.2 us -> 38.6 us
    pallas_call x1, Pallas kernels: 38.2 us -> 37.6 us  [per_device(): pl.pallas_call(functools.partial(kernel, groups, rows), out_shape=tuple(c...]
where the time goes in v6:
time: 39.3 us; the launch traced here: 39.2 us
  Pallas kernels  38.6 us (98%)
  between operations  0.64 us (2%)
    pallas_call x1, Pallas kernels, per_device(): pl.pallas_call(functools.partial(kernel, groups, rows), out_shape=tuple(c...  37.6 us
    pallas_call x1, Pallas kernels, per_device(): pl.pallas_call(write_kernel, out_shape=found, in_specs=[vmem] * 5, out_sp...  1.03 us

profile of v6, /device:TPU:1, one launch (start us, length us, event | category | flops | bytes accessed | tf_op | source)
XLA Modules:
  0.0 39.2 jit_solution(14852482369349319426)
XLA Ops:
  0.6 37.6 %shard_map.120 = (f32[32,8,128]{2,1,0:T(8,128)S(1)}, f32[1,128]{1,0:T(1,128)S(1)}, f32[32,8,128]{2,1,0:T(8,128)S(1)}, f32[32,8,128]{2,1,0:T(8,128)S(1)}, f32[3,40,8,128]{3,2,1,0:T(8,128)S(1)}) custom-call(f32[32,8,128]{2,1,0:T(8,128)} %vt_hbm.1, f32[32,8,128]{2,1,0:T(8,128)} %wb_hbm.1, f32[32,8,128]{2,1,0:T(8,128)} %wn_hbm.1, f32[32,8,128]{2,1,0:T(8,128)} %al_hbm.1, ...), custom_call_target="tpu_custom_call" | custom-call | tf_op jit(solution)/shard_map/pallas_call | solution.py:703
  38.2 1.0 %shard_map.121 = (f32[32,8,128]{2,1,0:T(8,128)}, f32[1,128]{1,0:T(1,128)}, f32[32,8,128]{2,1,0:T(8,128)}, f32[32,8,128]{2,1,0:T(8,128)}) custom-call(f32[32,8,128]{2,1,0:T(8,128)S(1)} %get-tuple-element.13.gv_ref, f32[1,128]{1,0:T(1,128)S(1)} %get-tuple-element.14.gc_ref, f32[32,8,128]{2,1,0:T(8,128)S(1)} %get-tuple-element.15.am_ref, ...), custom_call_target="tpu_custom_call" | custom-call | tf_op jit(solution)/shard_map/pallas_call | solution.py:762
